TPU v7x, 512 devices: a whole 4x4x16 slice. The times are simulated.
512 devices in a mesh: dp: 32 (over z, core), tp: 16 (over x, y).
Axes of the slice: x: 4, y: 4, z: 16, core: 2. Of those that a mesh axis runs over, the one named last changes fastest.
Arguments:
- tokens: bfloat16 [16384, 2048], P(('dp', 'tp')), may hold values from -6 to 6
- norm_gain: float32 [2048], replicated, may hold values from 0.5 to 1.5
- w_query: bfloat16 [2048, 2048], P('dp', 'tp'), may hold values from -0.125 to 0.125
- w_key: bfloat16 [2048, 2048], P('dp', 'tp'), may hold values from -0.125 to 0.125
- w_value: bfloat16 [2048, 4096], P('dp', 'tp'), may hold values from -0.125 to 0.125
- w_gate: bfloat16 [2048, 4096], P('dp', 'tp'), may hold values from -0.125 to 0.125
- w_beta: bfloat16 [2048, 32], P('dp', 'tp'), may hold values from -0.125 to 0.125
- w_decay: bfloat16 [2048, 32], P('dp', 'tp'), may hold values from -0.125 to 0.125
- conv_query: float32 [4, 2048], P(None, 'tp'), may hold values from -3 to 3
- conv_key: float32 [4, 2048], P(None, 'tp'), may hold values from -3 to 3
- conv_value: float32 [4, 4096], P(None, 'tp'), may hold values from -3 to 3
- decay_rate: float32 [32], P('tp'), may hold values from 0.004 to 0.04
- dt_bias: float32 [32], P('tp'), may hold values from -1 to 1
- out_gain: float32 [128], replicated, may hold values from 0.5 to 1.5
- seg_ids: int32 [32, 512], P('dp'), may hold values from 0 to 15, never falling along the last dimension, each value on 1 to 128 neighbouring positions
Outputs:
- mixed_tiles: bfloat16 [16384, 4096], P(('dp', 'tp'))
Inputs may be any that keep to these rules, and one draw needn't show every extreme that they name: Each row of seg_ids never falls; every prompt covers 1 to 128 consecutive positions.
All inputs are finite; a program needn't handle non-finite values.
Results may differ from a plain program's by a relative error of at most 0.0034.
The roundings to bfloat16 on the way count: a program that leaves them out, or rounds other values in their place, can miss the bound.
Values may be sent and summed in bfloat16 or wider, within the bound.
No kernel may reach another device: no remote copies, remote signals or barrier semaphores. Data moves between devices by JAX's collectives and lax.ppermute only.
A program may use at most 64 MiB of HBM per device.

v0:
```python
import jax
import jax.numpy as jnp
from jax import lax
from jax.sharding import PartitionSpec as P

DK = 128
DV = 128
SPAN = 64


highest = lax.Precision.HIGHEST


def rms_rows(tokens, gain):
    floats = tokens.astype(jnp.float32)
    scaled = floats * lax.rsqrt(jnp.mean(floats * floats, axis=-1, keepdims=True) + 1e-06)
    return (scaled * gain).astype(jnp.bfloat16)


def split_columns(projected, column_counts):
    pieces = []
    offset = 0
    for count in column_counts:
        pieces.append(projected[:, offset : offset + count])
        offset = offset + count
    return pieces


def causal_conv(projected, kernel, segment):
    kernel_len = kernel.shape[0]
    summed = projected * kernel[kernel_len - 1]
    for offset in range(1, kernel_len):
        zeros_top = jnp.zeros((offset, projected.shape[1]), jnp.float32)
        shifted = jnp.concatenate([zeros_top, projected[:-offset]], axis=0)
        earlier = jnp.concatenate([jnp.full((offset,), -1, jnp.int32), segment[:-offset]])
        same_doc = (earlier == segment).astype(jnp.float32)
        summed = summed + shifted * same_doc[:, None] * kernel[kernel_len - 1 - offset]
    return jax.nn.silu(summed)


def unit_heads(values, heads, head_size):
    shaped = values.reshape(values.shape[0], heads, head_size)
    return shaped * lax.rsqrt(jnp.sum(shaped * shaped, axis=-1, keepdims=True) + 1e-06)


def delta_head(query, key_rows, value, beta, log_decay, segment):
    row_count = query.shape[0]
    blocks = row_count // SPAN
    value_size = value.shape[1]
    q_blocks = query.reshape(blocks, SPAN, query.shape[1])
    k_blocks = key_rows.reshape(blocks, SPAN, key_rows.shape[1])
    v_blocks = value.reshape(blocks, SPAN, value_size)
    beta_blocks = beta.reshape(blocks, SPAN)
    decay_blocks = log_decay.reshape(blocks, SPAN)
    seg_blocks = segment.reshape(blocks, SPAN)
    before = jnp.concatenate([jnp.full((1,), -1, jnp.int32), seg_blocks[:-1, -1]])
    row_index = lax.broadcasted_iota(jnp.int32, (SPAN, SPAN), 0)
    col_index = lax.broadcasted_iota(jnp.int32, (SPAN, SPAN), 1)
    lower_mask = row_index >= col_index
    strict = row_index > col_index

    def advance(state, inputs):
        block_q, block_k, block_v, block_beta, block_decay, block_seg, block_before = inputs
        cumulative = jnp.cumsum(block_decay)
        same_doc = block_seg[:, None] == block_seg[None, :]
        spread = jnp.where(lower_mask, cumulative[:, None] - cumulative[None, :], 0.0)
        decay_matrix = jnp.where(lower_mask & same_doc, jnp.exp(spread), 0.0)
        carried = (block_seg == block_before).astype(jnp.float32)
        from_start = jnp.exp(cumulative) * carried
        key_gram = jnp.dot(block_k, block_k.T, precision=highest)
        lower_matrix = jnp.where(strict, block_beta[:, None] * key_gram * decay_matrix, 0.0)
        system = jnp.eye(SPAN, dtype=jnp.float32) + lower_matrix
        right_side = jnp.concatenate(
            [block_beta[:, None] * block_v, (block_beta * from_start)[:, None] * block_k], axis=1
        )
        solved = lax.linalg.triangular_solve(
            system, right_side, left_side=True, lower=True, unit_diagonal=True
        )
        updates = solved[:, :value_size] - jnp.dot(solved[:, value_size:], state, precision=highest)
        scores = jnp.dot(block_q, block_k.T, precision=highest) * decay_matrix
        output = jnp.dot(from_start[:, None] * block_q, state, precision=highest) + jnp.dot(
            scores, updates, precision=highest
        )
        tail_weight = jnp.where(
            block_seg == block_seg[-1], jnp.exp(cumulative[-1] - cumulative), 0.0
        )
        new_state = jnp.exp(cumulative[-1]) * carried[-1] * state + jnp.dot(
            (tail_weight[:, None] * block_k).T, updates, precision=highest
        )
        return (new_state, output)

    initial = jnp.zeros((key_rows.shape[1], value_size), jnp.float32)
    last_state, outputs = lax.scan(
        advance,
        initial,
        (q_blocks, k_blocks, v_blocks, beta_blocks, decay_blocks, seg_blocks, before),
    )
    return outputs.reshape(row_count, value_size)


def prepare_heads(parts, segment, conv_query, conv_key, conv_value, decay_rate, dt_bias):
    proj_query, proj_key, proj_value, proj_gate, proj_beta, proj_decay = [
        piece_part.astype(jnp.float32) for piece_part in parts
    ]
    key_heads = proj_query.shape[1] // DK
    value_heads = proj_value.shape[1] // DV
    repeat = value_heads // key_heads
    query = unit_heads(causal_conv(proj_query, conv_query, segment), key_heads, DK) * DK ** (-0.5)
    keys = unit_heads(causal_conv(proj_key, conv_key, segment), key_heads, DK)
    values = causal_conv(proj_value, conv_value, segment).reshape(
        proj_value.shape[0], value_heads, DV
    )
    query = jnp.repeat(query, repeat, axis=1)
    keys = jnp.repeat(keys, repeat, axis=1)
    beta = jax.nn.sigmoid(proj_beta)
    log_decay = -decay_rate * jax.nn.softplus(proj_decay + dt_bias)
    gate_act = jax.nn.silu(proj_gate.reshape(proj_gate.shape[0], value_heads, DV))
    return (query, keys, values, beta, log_decay, gate_act)


def finish_heads(mixed, gate_act, out_gain):
    normed = mixed * lax.rsqrt(jnp.mean(mixed * mixed, axis=-1, keepdims=True) + 1e-06) * out_gain
    return (normed * gate_act).astype(jnp.bfloat16)


def shards(
    tokens,
    norm_gain,
    w_query,
    w_key,
    w_value,
    w_gate,
    w_beta,
    w_decay,
    conv_query,
    conv_key,
    conv_value,
    decay_rate,
    dt_bias,
    out_gain,
    seg_ids,
):
    gathered = (
        lax.all_gather(w_query, "dp", axis=0, tiled=True),
        lax.all_gather(w_key, "dp", axis=0, tiled=True),
        lax.all_gather(w_value, "dp", axis=0, tiled=True),
        lax.all_gather(w_gate, "dp", axis=0, tiled=True),
        lax.all_gather(w_beta, "dp", axis=0, tiled=True),
        lax.all_gather(w_decay, "dp", axis=0, tiled=True),
    )
    column_counts = [matrix.shape[1] for matrix in gathered]
    joined = jnp.concatenate(gathered, axis=1)
    projected = jnp.dot(
        rms_rows(lax.all_gather(tokens, "tp", axis=0, tiled=True), norm_gain),
        joined,
        preferred_element_type=jnp.float32,
    ).astype(jnp.bfloat16)
    parts = split_columns(projected, column_counts)
    segment = seg_ids[0]
    query, keys, values, beta, log_decay, gate_act = prepare_heads(
        parts, segment, conv_query, conv_key, conv_value, decay_rate, dt_bias
    )
    row_count = values.shape[0]
    local_heads = values.shape[1]
    mixed = jax.vmap(delta_head, in_axes=(1, 1, 1, 1, 1, None), out_axes=1)(
        query, keys, values, beta, log_decay, segment
    )
    tiles = finish_heads(mixed, gate_act, out_gain).reshape(row_count, local_heads * DV)
    return lax.all_to_all(tiles, "tp", split_axis=0, concat_axis=1, tiled=True)


def solution(mesh):
    in_specs = (
        P(("dp", "tp"), None),
        P(),
        P("dp", "tp"),
        P("dp", "tp"),
        P("dp", "tp"),
        P("dp", "tp"),
        P("dp", "tp"),
        P("dp", "tp"),
        P(None, "tp"),
        P(None, "tp"),
        P(None, "tp"),
        P("tp"),
        P("tp"),
        P(),
        P("dp", None),
    )
    out_specs = P(("dp", "tp"), None)
    return jax.shard_map(shards, mesh=mesh, in_specs=in_specs, out_specs=out_specs, check_vma=False)
```

profile of v0, /device:TPU:1, one launch (start us, length us, event | category | flops | bytes accessed | tf_op | source)
XLA Modules:
  0.0 379.0 jit_solution(4862231805147400210)
XLA Ops:
  6.5 0.7 all-gather.8.cloned.1.call-update
  7.3 0.7 all-gather.10.cloned.1.call-update
  8.1 0.7 all-gather.6.cloned.1.call-update
  8.8 37.5 %all-gather = bf16[32,64,2]{1,2,0:T(2,128)(2,1)S(1)} all-gather(bf16[1,64,2]{1,2,0:T(2,128)(2,1)} %bitcast.187), channel_id=1, replica_groups=mesh['dp'=32,'tp'=16] {'dp'}, dimensions={0}, use_global_device_ids=true | all-gather | bytes 8448 | tf_op jit(solution)/shard_map/all_gather | solution.py:148
  46.6 27.0 %all-gather.1 = bf16[32,64,2]{1,2,0:T(2,128)(2,1)S(1)} all-gather(bf16[1,64,2]{1,2,0:T(2,128)(2,1)} %bitcast.188), channel_id=1, replica_groups=mesh['dp'=32,'tp'=16] {'dp'}, dimensions={0}, use_global_device_ids=true | all-gather | bytes 8448 | tf_op jit(solution)/shard_map/all_gather | solution.py:149
  74.0 0.7 neg.25
  75.2 1.3 reduce.11
  76.8 0.8 slice_bitcast_fusion.3
  77.6 0.8 slice_bitcast_fusion.7
  78.4 0.8 fusion.69
  79.3 0.9 fusion.65
  80.2 30.1 %all_gather.22 = bf16[2048,128]{1,0:T(8,128)(2,1)S(1)} all-gather(bf16[64,128]{1,0:T(8,128)(2,1)} %param.19), channel_id=1, replica_groups=mesh['dp'=32,'tp'=16] {'dp'}, dimensions={0}, use_global_device_ids=true | all-gather | bytes 540672 | tf_op jit(solution)/shard_map/all_gather | solution.py:144
  110.3 28.9 %all_gather.23 = bf16[2048,128]{1,0:T(8,128)(2,1)S(1)} all-gather(bf16[64,128]{1,0:T(8,128)(2,1)} %param.20), channel_id=1, replica_groups=mesh['dp'=32,'tp'=16] {'dp'}, dimensions={0}, use_global_device_ids=true | all-gather | bytes 540672 | tf_op jit(solution)/shard_map/all_gather | solution.py:145
  139.2 16.7 %all-gather.10.cloned.1.call-done = bf16[2048,256]{1,0:T(8,128)(2,1)} async-done(((bf16[64,256]{1,0:T(8,128)(2,1)}), bf16[2048,256]{1,0:T(8,128)(2,1)}) %all-gather.10.cloned.1.call-update) | async-done | bytes 1048592 | tf_op jit(solution)/shard_map/all_gather | solution.py:147
  156.0 6.4 %concatenate.57 = bf16[2048,772]{1,0:T(8,128)(2,1)} concatenate(bf16[2048,128]{1,0:T(8,128)(2,1)S(1)} %all_gather.22, bf16[2048,128]{1,0:T(8,128)(2,1)S(1)} %all_gather.23, bf16[2048,256]{1,0:T(8,128)(2,1)} %all-gather.8.cloned.1.call-done, bf16[2048,256]{1,0:T(8,128)(2,1)} %all-gather.10.cloned.1.call-done, bf16[2048,2]{1,0:T(8,128)(2,1)S(1)} %bitcast.171, ...), dimensions={1} | concatenate | bytes 6324224 | tf_op jit(solution)/shard_map/concatenate | solution.py:152
  162.4 52.7 %all-gather.6.cloned.1.call-done = bf16[512,2048]{1,0:T(8,128)(2,1)} async-done(((bf16[32,2048]{1,0:T(8,128)(2,1)}), bf16[512,2048]{1,0:T(8,128)(2,1)}) %all-gather.6.cloned.1.call-update) | async-done | bytes 2097168 | tf_op jit(solution)/shard_map/all_gather | solution.py:154
  215.1 2.1 fusion.47
  217.2 4.7 %fusion.54 = bf16[512,772]{0,1:T(8,128)(2,1)S(1)} fusion(bf16[2048,772]{1,0:T(8,128)(2,1)} %concatenate.57, bf16[512,2048]{1,0:T(8,128)(2,1)} %all-gather.6.cloned.1.call-done, f32[2048]{0:T(1024)S(1)} %copy-done.2, f32[512]{0:T(512)S(1)} %add_rsqrt_fusion.3), kind=kOutput, calls=%fused_computation.80 | convolution fusion | flops 1623590912 | bytes 6060032 | tf_op jit(solution)/shard_map/dot_general | solution.py:153
  222.3 0.7 multiply_reduce_fusion
  223.2 0.7 divide_multiply_fusion
  224.4 134.5 %while.14 = (s32[]{:T(128)}, f32[2,128,128]{2,1,0:T(8,128)S(1)}, f32[8,2,64,128]{3,2,0,1:T(8,128)S(1)}, f32[8,2,64]{2,1,0:T(2,128)S(1)}, s32[8,64]{1,0:T(8,128)S...) while((s32[]{:T(128)}, f32[2,128,128]{2,1,0:T(8,128)S(1)}, ...), condition=%wide.region_5.6_spmd.clone.clone, body=%wide.region_3.5_spmd.clone.clone.sunk | while | flops 138863296 | bytes 2245832 | solution.py:93
  228.7 9.8 %custom-call.8 = f32[2,1,64,64]{2,3,1,0:T(8,128)S(1)} custom-call(f32[2,1,64,64]{3,2,1,0:T(8,128)S(1)} %fusion.108), custom_call_target="InvertDiagBlocksLowerTriangular" | custom-call | tf_op jit(solution)/shard_map/vmap()/while/body/eval_jaxpr/triangular_solve | solution.py:76
  241.2 0.6 dynamic_slice.85
  245.5 9.8 %custom-call.8 = f32[2,1,64,64]{2,3,1,0:T(8,128)S(1)} custom-call(f32[2,1,64,64]{3,2,1,0:T(8,128)S(1)} %fusion.108), custom_call_target="InvertDiagBlocksLowerTriangular" | custom-call | tf_op jit(solution)/shard_map/vmap()/while/body/eval_jaxpr/triangular_solve | solution.py:76
  262.3 9.8 %custom-call.8 = f32[2,1,64,64]{2,3,1,0:T(8,128)S(1)} custom-call(f32[2,1,64,64]{3,2,1,0:T(8,128)S(1)} %fusion.108), custom_call_target="InvertDiagBlocksLowerTriangular" | custom-call | tf_op jit(solution)/shard_map/vmap()/while/body/eval_jaxpr/triangular_solve | solution.py:76
  279.1 9.8 %custom-call.8 = f32[2,1,64,64]{2,3,1,0:T(8,128)S(1)} custom-call(f32[2,1,64,64]{3,2,1,0:T(8,128)S(1)} %fusion.108), custom_call_target="InvertDiagBlocksLowerTriangular" | custom-call | tf_op jit(solution)/shard_map/vmap()/while/body/eval_jaxpr/triangular_solve | solution.py:76
  295.9 9.8 %custom-call.8 = f32[2,1,64,64]{2,3,1,0:T(8,128)S(1)} custom-call(f32[2,1,64,64]{3,2,1,0:T(8,128)S(1)} %fusion.108), custom_call_target="InvertDiagBlocksLowerTriangular" | custom-call | tf_op jit(solution)/shard_map/vmap()/while/body/eval_jaxpr/triangular_solve | solution.py:76
  312.7 9.8 %custom-call.8 = f32[2,1,64,64]{2,3,1,0:T(8,128)S(1)} custom-call(f32[2,1,64,64]{3,2,1,0:T(8,128)S(1)} %fusion.108), custom_call_target="InvertDiagBlocksLowerTriangular" | custom-call | tf_op jit(solution)/shard_map/vmap()/while/body/eval_jaxpr/triangular_solve | solution.py:76
  329.6 9.8 %custom-call.8 = f32[2,1,64,64]{2,3,1,0:T(8,128)S(1)} custom-call(f32[2,1,64,64]{3,2,1,0:T(8,128)S(1)} %fusion.108), custom_call_target="InvertDiagBlocksLowerTriangular" | custom-call | tf_op jit(solution)/shard_map/vmap()/while/body/eval_jaxpr/triangular_solve | solution.py:76
  346.4 9.8 %custom-call.8 = f32[2,1,64,64]{2,3,1,0:T(8,128)S(1)} custom-call(f32[2,1,64,64]{3,2,1,0:T(8,128)S(1)} %fusion.108), custom_call_target="InvertDiagBlocksLowerTriangular" | custom-call | tf_op jit(solution)/shard_map/vmap()/while/body/eval_jaxpr/triangular_solve | solution.py:76
  360.0 11.8 %all_to_all.19 = bf16[16,32,256]{2,1,0:T(8,128)(2,1)S(1)} all-to-all(bf16[16,32,256]{2,1,0:T(8,128)(2,1)S(1)} %all_to_all.14), channel_id=1, replica_groups=mesh['dp'=32,'tp'=16] {'tp'}, dimensions={0} | all-to-all | bytes 524288 | tf_op jit(solution)/shard_map/all_to_all | solution.py:169
  371.8 0.7 copy.90
  (222 shorter events, 53.3 us)
Async XLA Ops:
  6.5 132.7 %all-gather.8.cloned.1.call-start = ((), (), s32[]{:S(2)}) async-start(), calls=%async_computation.2 | async-start | bytes 1081344 | tf_op jit(solution)/shard_map/all_gather | solution.py:146
  7.3 148.7 %all-gather.10.cloned.1.call-start = ((), (), s32[]{:S(2)}) async-start(), calls=%async_computation.3 | async-start | bytes 1081344 | tf_op jit(solution)/shard_map/all_gather | solution.py:147
  8.0 207.1 %all-gather.6.cloned.1.call-start = ((), (), s32[]{:S(2)}) async-start(), calls=%async_computation.1 | async-start | bytes 2228224 | tf_op jit(solution)/shard_map/all_gather | solution.py:154
  156.0 61.2 %copy-start.2 = (f32[2048]{0:T(1024)S(1)}, f32[2048]{0:T(1024)}, u32[]{:S(2)}) copy-start(f32[2048]{0:T(1024)} %param.18) | copy-start | bytes 24580
  217.2 4.9 %copy-start.1 = (f32[2]{0:T(128)S(1)}, f32[2]{0:T(128)}, u32[]{:S(2)}) copy-start(f32[2]{0:T(128)} %param.29) | copy-start | bytes 28
  224.4 134.9 %copy-start = (f32[128]{0:T(128)S(1)}, f32[128]{0:T(128)}, u32[]{:S(2)}) copy-start(f32[128]{0:T(128)} %param.30) | copy-start | bytes 1540
Sparse Core Ops, SparseCore 0:
  9.5 76.3 all-gather.7
  88.0 67.9 all-gather.9
  159.0 56.0 all-gather.5
where the time goes:
time: 381 us; the launch traced here: 379 us
  blocking collectives  135 us (35%)
  other arithmetic  104 us (27%)
  waiting for transfers between devices  71.5 us (19%)
  local copies, waits for them, and re-layouts  27.8 us (7%)
  matrix products  21.2 us (6%)
  between operations  13.3 us (3%)
  loops' own time  5.55 us (1%)
    another operation x32, other arithmetic, advance(): lax.linalg.triangular_solve(system, right_side, left_side=True, lower=Tru...  80 us
    all_gather x1, waiting for transfers between devices, shards(): lax.all_gather(tokens, 'tp', axis=0, tiled=True)  52.7 us
    all_gather x1, blocking collectives, shards(): lax.all_gather(w_beta, 'dp', axis=0, tiled=True)  37.5 us
    all_gather x1, blocking collectives, shards(): lax.all_gather(w_query, 'dp', axis=0, tiled=True)  30.1 us
    all_gather x1, blocking collectives, shards(): lax.all_gather(w_key, 'dp', axis=0, tiled=True)  28.9 us
    all_gather x1, blocking collectives, shards(): lax.all_gather(w_decay, 'dp', axis=0, tiled=True)  27 us
    all_gather x1, waiting for transfers between devices, shards(): lax.all_gather(w_gate, 'dp', axis=0, tiled=True)  16.7 us
    all_to_all x1, blocking collectives, shards(): return lax.all_to_all(tiles, 'tp', split_axis=0, concat_axis=1, tiled=True)  11.8 us
  transfers between devices with their start and end apart: 3, of which 2 were waited for; matrix products, arithmetic and copies ran while one was open for 4% of the time, Pallas kernels for 0%

commit v1 on v0

v1 whole, which is shorter than its diff:
```python
import jax
import jax.numpy as jnp
from jax import lax
from jax.experimental import pallas as pl
from jax.experimental.pallas import tpu as pltpu
from jax.sharding import PartitionSpec as P

BLOCK = 128
BASE = 16


def split_two(x):
    high = x.astype(jnp.bfloat16)
    low = (x - high.astype(jnp.float32)).astype(jnp.bfloat16)
    return high, low


def dot_split(a, b):
    ah, al = split_two(a)
    bh, bl = split_two(b)
    return jnp.dot(
        jnp.concatenate([ah, al, ah], axis=1),
        jnp.concatenate([bh, bh, bl], axis=0),
        preferred_element_type=jnp.float32,
    )


def iota(shape, axis):
    return lax.broadcasted_iota(jnp.int32, shape, axis)


def silu(x):
    return x / (1.0 + jnp.exp(-x))


def softplus(x):
    return jnp.maximum(x, 0.0) + jnp.log1p(jnp.exp(-jnp.abs(x)))


def columns_of(rows):
    filled = jnp.concatenate(
        [rows, jnp.zeros((128 - rows.shape[0], rows.shape[1]), jnp.float32)], axis=0
    )
    return filled.T


def conv_silu(p, taps, masks):
    summed = p * taps[3:4, :]
    for offset in range(1, 4):
        shifted = pltpu.roll(p, offset, 0)
        summed = summed + shifted * masks[offset - 1] * taps[3 - offset : 4 - offset, :]
    return silu(summed)


def unit(x):
    return x * lax.rsqrt(jnp.sum(x * x, axis=-1, keepdims=True) + 1e-06)


def mix_kernel(
    rate_ref, bias_ref, x0_ref, x1_ref, x2_ref, x3_ref, w_ref, seg_ref, tq_ref, tk_ref, tv_ref, gain_ref,
    out_ref, x_ref, p_ref
):
    rows = p_ref.shape[0]
    quarter = rows // 4
    mine = lax.axis_index("tp") // 4
    for ref, behind in ((x0_ref, 0), (x1_ref, 1), (x2_ref, 2), (x3_ref, 3)):
        place = lax.rem(mine + 4 - behind, 4)
        x_ref[pl.ds(pl.multiple_of(place * quarter, quarter), quarter), :] = ref[...]
    p_ref[...] = jnp.dot(x_ref[...], w_ref[...], preferred_element_type=jnp.float32).astype(jnp.bfloat16)
    blocks = rows // BLOCK
    seg_row = seg_ref[...].astype(jnp.float32)
    position = iota((1, rows), 1)
    masks = []
    for offset in range(1, 4):
        earlier = pltpu.roll(jnp.broadcast_to(seg_row, (8, rows)), offset, 1)[0:1]
        masks.append(jnp.where((position >= offset) & (earlier == seg_row), 1.0, 0.0))

    ba = p_ref[:, 768:896].astype(jnp.float32).T
    beta = 1.0 / (1.0 + jnp.exp(-ba[0:2]))
    rate = jnp.where(iota((2, 1), 0) == 0, rate_ref[0], rate_ref[1])
    bias = jnp.where(iota((2, 1), 0) == 0, bias_ref[0], bias_ref[1])
    decay = -rate * softplus(ba[2:4] + bias)
    upper = (iota((BLOCK, BLOCK), 0) <= iota((BLOCK, BLOCK), 1)).astype(jnp.bfloat16)
    decay_wide = jnp.concatenate([decay, jnp.zeros((6, rows), jnp.float32)], axis=0)
    stacked = jnp.concatenate(
        [decay_wide[:, b * BLOCK : (b + 1) * BLOCK] for b in range(blocks)], axis=0
    )
    high, low = split_two(stacked)
    lowest = (stacked - high.astype(jnp.float32) - low.astype(jnp.float32)).astype(jnp.bfloat16)
    total = jnp.dot(
        jnp.concatenate([high, low, lowest], axis=1),
        jnp.concatenate([upper, upper, upper], axis=0),
        preferred_element_type=jnp.float32,
    )
    cumulative, start, tail = [], [], []
    for b in range(blocks):
        part = total[8 * b : 8 * b + 2]
        seg_part = seg_row[:, b * BLOCK : (b + 1) * BLOCK]
        if b == 0:
            carried = jnp.zeros((1, BLOCK), jnp.float32)
        else:
            carried = jnp.where(seg_part == seg_row[:, b * BLOCK - 1 : b * BLOCK], 1.0, 0.0)
        closing = jnp.where(seg_part == seg_part[:, BLOCK - 1 :], 1.0, 0.0)
        cumulative.append(part)
        start.append(jnp.exp(part) * carried)
        tail.append(jnp.exp(part[:, BLOCK - 1 :] - part) * closing)
    cumulative = jnp.concatenate(cumulative, axis=1)
    start = jnp.concatenate(start, axis=1)
    tail = jnp.concatenate(tail, axis=1)
    cols = columns_of(
        jnp.concatenate([beta, cumulative, start, tail, beta * start, seg_row] + masks, axis=0)
    )
    mask_cols = [cols[:, 11 + i : 12 + i] for i in range(3)]

    query = unit(conv_silu(p_ref[:, 0:128].astype(jnp.float32), tq_ref[...], mask_cols)) * 128 ** (-0.5)
    key = unit(conv_silu(p_ref[:, 128:256].astype(jnp.float32), tk_ref[...], mask_cols))
    values = [
        conv_silu(
            p_ref[:, 256 + 128 * h : 384 + 128 * h].astype(jnp.float32),
            tv_ref[:, 128 * h : 128 * (h + 1)],
            mask_cols,
        )
        for h in range(2)
    ]

    row_at = iota((BLOCK, BLOCK), 0)
    col_at = iota((BLOCK, BLOCK), 1)
    base_diagonal = (row_at // BASE) == (col_at // BASE)
    picks = jnp.concatenate(
        [((row_at // BASE == col_at // BASE) & (row_at % BASE == j)).astype(jnp.bfloat16) for j in range(BASE - 1)],
        axis=1,
    )
    picks = jnp.concatenate([picks, picks], axis=0)

    problems = [(b, h) for b in range(blocks) for h in range(2)]
    scores, lowers, packed = {}, {}, []
    for b in range(blocks):
        span = slice(b * BLOCK, (b + 1) * BLOCK)
        k_b = key[span]
        grams = dot_split(jnp.concatenate([k_b, query[span]], axis=0), k_b.T)
        same = cols[span, 10:11] == seg_row[:, span]
        for h in range(2):
            spread = jnp.where(row_at >= col_at, cols[span, 2 + h : 3 + h] - cumulative[h : h + 1, span], 0.0)
            matrix = jnp.where((row_at >= col_at) & same, jnp.exp(spread), 0.0)
            scores[b, h] = grams[BLOCK:] * matrix
            lowers[b, h] = jnp.where(
                row_at > col_at, cols[span, h : h + 1] * grams[:BLOCK] * matrix, 0.0
            )
            masked = jnp.where(base_diagonal, lowers[b, h], 0.0)
            slab = masked[0:BASE]
            for d in range(1, BLOCK // BASE):
                slab = slab + masked[d * BASE : (d + 1) * BASE]
            packed.append(slab)
    high, low = split_two(jnp.concatenate(packed, axis=0))
    spread_columns = jnp.dot(
        jnp.concatenate([high, low], axis=1), picks, preferred_element_type=jnp.float32
    )
    unit_rows = (iota((BASE, BLOCK), 0) == iota((BASE, BLOCK), 1) % BASE).astype(jnp.float32)
    inverses = []
    for i in range(len(problems)):
        solved = unit_rows
        for j in range(BASE - 1):
            factor = spread_columns[i * BASE : (i + 1) * BASE, j * BLOCK : (j + 1) * BLOCK]
            solved = solved - factor * solved[j : j + 1]
        inverses.append(solved)

    first, state = {}, {}
    for i, (b, h) in enumerate(problems):
        span = slice(b * BLOCK, (b + 1) * BLOCK)
        inverse = jnp.where(base_diagonal, jnp.concatenate([inverses[i]] * (BLOCK // BASE), axis=0), 0.0)
        size = BASE
        while size < BLOCK:
            below = (row_at // (2 * size) == col_at // (2 * size)) & (row_at // size != col_at // size)
            off = jnp.where(below, lowers[b, h], 0.0)
            inverse = inverse - dot_split(dot_split(inverse, off), inverse)
            size = 2 * size
        right = jnp.concatenate(
            [cols[span, h : h + 1] * values[h][span], cols[span, 8 + h : 9 + h] * key[span]], axis=1
        )
        solved = dot_split(inverse, right)
        first[b, h] = solved
        if b < blocks - 1:
            state[b + 1, h] = dot_split((cols[span, 6 + h : 7 + h] * key[span]).T, solved[:, :128])
    gain = gain_ref[...]
    for b, h in problems:
        span = slice(b * BLOCK, (b + 1) * BLOCK)
        update = first[b, h][:, :128]
        if b > 0:
            both = dot_split(
                jnp.concatenate([first[b, h][:, 128:], cols[span, 4 + h : 5 + h] * query[span]], axis=0),
                state[b, h],
            )
            update = update - both[:BLOCK]
            mixed = both[BLOCK:] + dot_split(scores[b, h], update)
        else:
            mixed = dot_split(scores[b, h], update)
        normed = mixed * lax.rsqrt(jnp.mean(mixed * mixed, axis=-1, keepdims=True) + 1e-06) * gain
        gate = silu(p_ref[span, 512 + 128 * h : 640 + 128 * h].astype(jnp.float32))
        out_ref[span, 128 * h : 128 * (h + 1)] = (normed * gate).astype(jnp.bfloat16)


def rms_rows(tokens, gain):
    floats = tokens.astype(jnp.float32)
    scaled = floats * lax.rsqrt(jnp.mean(floats * floats, axis=-1, keepdims=True) + 1e-06)
    return (scaled * gain).astype(jnp.bfloat16)


def shards(
    tokens,
    norm_gain,
    w_query,
    w_key,
    w_value,
    w_gate,
    w_beta,
    w_decay,
    conv_query,
    conv_key,
    conv_value,
    decay_rate,
    dt_bias,
    out_gain,
    seg_ids,
):
    joined = jnp.concatenate(
        [w_query, w_key, w_value, w_gate, w_beta, w_decay, jnp.zeros((w_beta.shape[0], 124), jnp.bfloat16)], axis=1
    )
    weights = lax.all_gather(joined, "dp", axis=0, tiled=True)
    normed = rms_rows(tokens, norm_gain)
    lines = [[4 * x + y for y in range(4)] for x in range(4)]
    quarter = lax.all_gather(normed, "tp", axis=0, tiled=True, axis_index_groups=lines)

    def from_behind(shift):
        return lax.ppermute(quarter, "tp", [(i, (i + 4 * shift) % 16) for i in range(16)])

    rows = [quarter, from_behind(1), from_behind(2), from_behind(3)]
    vmem = pl.BlockSpec(memory_space=pltpu.VMEM)
    smem = pl.BlockSpec(memory_space=pltpu.SMEM)
    tiles = pl.pallas_call(
        mix_kernel,
        out_shape=jax.ShapeDtypeStruct((512, 256), jnp.bfloat16),
        in_specs=[smem, smem] + [vmem] * 10,
        out_specs=vmem,
        scratch_shapes=[pltpu.VMEM((512, 2048), jnp.bfloat16), pltpu.VMEM((512, 896), jnp.bfloat16)],
        compiler_params=pltpu.CompilerParams(vmem_limit_bytes=40 * 1024 * 1024),
    )(decay_rate, dt_bias, *rows, weights, seg_ids, conv_query, conv_key, conv_value, out_gain.reshape(1, 128))
    return lax.all_to_all(tiles, "tp", split_axis=0, concat_axis=1, tiled=True)


def solution(mesh):
    in_specs = (
        P(("dp", "tp"), None),
        P(),
        P("dp", "tp"),
        P("dp", "tp"),
        P("dp", "tp"),
        P("dp", "tp"),
        P("dp", "tp"),
        P("dp", "tp"),
        P(None, "tp"),
        P(None, "tp"),
        P(None, "tp"),
        P("tp"),
        P("tp"),
        P(),
        P("dp", None),
    )
    out_specs = P(("dp", "tp"), None)
    return jax.shard_map(shards, mesh=mesh, in_specs=in_specs, out_specs=out_specs, check_vma=False)
```

time: 381 us -> 132 us (0.35)
  blocking collectives: 135 us -> 25.2 us
  other arithmetic: 104 us -> 2.06 us
  matrix products: 21.2 us -> 0 us
  local copies, waits for them, and re-layouts: 27.8 us -> 10.5 us
  waiting for transfers between devices: 71.5 us -> 55.4 us
  Pallas kernels: 0 us -> 13.9 us
  starting transfers between devices: 0.08 us -> 10.7 us
  loops' own time: 5.55 us -> 0 us
    all_gather x4 -> x1, blocking collectives: 124 us -> 11.2 us  [shards(): lax.all_gather(normed, 'tp', axis=0, tiled=True, axis_index_groups=lines)]
    another operation x40 -> x0, other arithmetic: 81.9 us -> none  [the longest x32 80 us: advance(): lax.linalg.triangular_solve(system, right_side, left_side=True, lower=Tru...]
    all_gather x3 -> x1, waiting for transfers between devices: 69.4 us -> 32.8 us  [shards(): weights = lax.all_gather(joined, 'dp', axis=0, tiled=True)]
    ppermute x0 -> x3, waiting for transfers between devices: none -> 22.5 us  [from_behind(): lax.ppermute(quarter, 'tp', [(i, (i + 4 * shift) % 16) for i in range(16)])]
    dot_general x49 -> x0, matrix products: 18.6 us -> none  [the longest x1 4.72 us: shards(): jnp.dot(rms_rows(lax.all_gather(tokens, 'tp', axis=0, tiled=True), norm_g...]
    pallas_call x0 -> x1, Pallas kernels: none -> 13.9 us  [shards(): pl.pallas_call(mix_kernel, out_shape=jax.ShapeDtypeStruct((512, 256), jnp...]
    slice x26 -> x0, local copies, waits for them, and re-layouts: 11.7 us -> none  [the longest x8 4.62 us: advance(): carried[-1]]
    ppermute x0 -> x3, starting transfers between devices: none -> 10.7 us  [from_behind(): lax.ppermute(quarter, 'tp', [(i, (i + 4 * shift) % 16) for i in range(16)])]
  transfers between devices with their start and end apart: 3 -> 4, of which waited for: 2 -> 4; matrix products, arithmetic and copies ran while one was open for 4% -> 2% of each run, Pallas kernels for 0% -> 0%
where the time goes in v1:
time: 132 us; the launch traced here: 131 us
  waiting for transfers between devices  55.4 us (42%)
  blocking collectives  25.2 us (19%)
  Pallas kernels  13.9 us (11%)
  between operations  13.4 us (10%)
  starting transfers between devices  10.7 us (8%)
  local copies, waits for them, and re-layouts  10.5 us (8%)
  other arithmetic  2.06 us (2%)
    all_gather x1, waiting for transfers between devices, shards(): weights = lax.all_gather(joined, 'dp', axis=0, tiled=True)  32.8 us
    ppermute x3, waiting for transfers between devices, from_behind(): lax.ppermute(quarter, 'tp', [(i, (i + 4 * shift) % 16) for i in range(16)])  22.5 us
    all_to_all x1, blocking collectives, shards(): return lax.all_to_all(tiles, 'tp', split_axis=0, concat_axis=1, tiled=True)  14 us
    pallas_call x1, Pallas kernels, shards(): pl.pallas_call(mix_kernel, out_shape=jax.ShapeDtypeStruct((512, 256), jnp...  13.9 us
    all_gather x1, blocking collectives, shards(): lax.all_gather(normed, 'tp', axis=0, tiled=True, axis_index_groups=lines)  11.2 us
    ppermute x3, starting transfers between devices, from_behind(): lax.ppermute(quarter, 'tp', [(i, (i + 4 * shift) % 16) for i in range(16)])  10.7 us
    unnamed x18, local copies, waits for them, and re-layouts  8.25 us
  transfers between devices with their start and end apart: 4, of which 4 were waited for; matrix products, arithmetic and copies ran while one was open for 2% of the time, Pallas kernels for 0%

profile of v1, /device:TPU:1, one launch (start us, length us, event | category | flops | bytes accessed | tf_op | source)
XLA Modules:
  0.0 131.2 jit_solution(11053011485655703473)
XLA Ops:
  6.5 0.0 all-gather.2.cloned.1.call-start
  6.5 0.8 copy.16
  7.3 0.8 copy.17
  8.1 1.5 %concatenate.3 = bf16[64,896]{1,0:T(8,128)(2,1)} concatenate(bf16[64,128]{1,0:T(8,128)(2,1)} %param.17, bf16[64,128]{1,0:T(8,128)(2,1)} %param.18, bf16[64,256]{1,0:T(8,128)(2,1)} %param.19, bf16[64,256]{1,0:T(8,128)(2,1)} %param.20, bf16[64,2]{1,0:T(8,128)(2,1)S(1)} %copy.16, bf16[64,2]{1,0:T(8,128)(2,1)S(1)} %copy.17, bf16[64,124]{1,0:T(8,128)(2,1)S(1)} %broadcast_in_dim.2), dimensions={1} | concatenate | bytes 229376 | tf_op jit(solution)/shard_map/concatenate | solution.py:225
  9.6 0.0 all-gather.2.cloned.1.call-update
  9.6 1.0 fusion
  10.7 1.0 fusion.2
  11.7 11.2 %all_gather.6.x0_ref = bf16[128,2048]{1,0:T(8,128)(2,1)S(1)} all-gather(bf16[32,2048]{1,0:T(8,128)(2,1)S(1)} %fusion.2), channel_id=1, replica_groups={{0,1,2,3},{4,5,6,7},{8,9,10,11},{12,13,14,15},{16,17,18,19},{20,21,22,2..., dimensions={0}, use_global_device_ids=true | all-gather | bytes 655360 | tf_op jit(solution)/shard_map/all_gather | solution.py:231
  22.9 5.7 %collective-permute-start.2 = (bf16[128,2048]{1,0:T(8,128)(2,1)S(1)}, bf16[128,2048]{1,0:T(8,128)(2,1)S(1)}, u32[]{:S(2)}, u32[]{:S(2)}) collective-permute-start(bf16[128,2048]{1,0:T(8,128)(2,1)S(1)} %all_gather.6.x0_ref), channel_id=1, source_target_pairs={{0,12},{1,13},{2,14},{3,15},{4,0},{5,1},{6,2},{7,3},{8,4},{9,5},{1... | collective-permute-start | bytes 1572872 | tf_op jit(solution)/shard_map/ppermute | solution.py:234
  28.7 2.4 %collective-permute-start.1 = (bf16[128,2048]{1,0:T(8,128)(2,1)S(1)}, bf16[128,2048]{1,0:T(8,128)(2,1)S(1)}, u32[]{:S(2)}, u32[]{:S(2)}) collective-permute-start(bf16[128,2048]{1,0:T(8,128)(2,1)S(1)} %all_gather.6.x0_ref), channel_id=1, source_target_pairs={{0,8},{1,9},{2,10},{3,11},{4,12},{5,13},{6,14},{7,15},{8,0},{9,1},... | collective-permute-start | bytes 1572872 | tf_op jit(solution)/shard_map/ppermute | solution.py:234
  31.1 2.5 %collective-permute-start = (bf16[128,2048]{1,0:T(8,128)(2,1)S(1)}, bf16[128,2048]{1,0:T(8,128)(2,1)S(1)}, u32[]{:S(2)}, u32[]{:S(2)}) collective-permute-start(bf16[128,2048]{1,0:T(8,128)(2,1)S(1)} %all_gather.6.x0_ref), channel_id=1, source_target_pairs={{0,4},{1,5},{2,6},{3,7},{4,8},{5,9},{6,10},{7,11},{8,12},{9,13},{1... | collective-permute-start | bytes 1572872 | tf_op jit(solution)/shard_map/ppermute | solution.py:234
  33.7 7.0 %collective-permute-done.2.x3_ref = bf16[128,2048]{1,0:T(8,128)(2,1)S(1)} collective-permute-done((bf16[128,2048]{1,0:T(8,128)(2,1)S(1)}, bf16[128,2048]{1,0:T(8,128)(2,1)S(1)}, u32[]{:S(2)}, u32[]{:S(2)}) %collective-permute-start.2) | collective-permute-done | bytes 524320 | tf_op jit(solution)/shard_map/ppermute | solution.py:234
  40.7 0.3 collective-permute-done.1.x2_ref
  41.0 15.2 %collective-permute-done.x1_ref = bf16[128,2048]{1,0:T(8,128)(2,1)S(1)} collective-permute-done((bf16[128,2048]{1,0:T(8,128)(2,1)S(1)}, bf16[128,2048]{1,0:T(8,128)(2,1)S(1)}, u32[]{:S(2)}, u32[]{:S(2)}) %collective-permute-start) | collective-permute-done | bytes 524320 | tf_op jit(solution)/shard_map/ppermute | solution.py:234
  56.2 32.8 %all-gather.2.cloned.1.call-done.w_ref = bf16[2048,896]{1,0:T(8,128)(2,1)} async-done(((bf16[64,896]{1,0:T(8,128)(2,1)}), bf16[2048,896]{1,0:T(8,128)(2,1)}) %all-gather.2.cloned.1.call-update) | async-done | bytes 3670032 | tf_op jit(solution)/shard_map/all_gather | solution.py:228
  89.0 0.0 copy-start
  89.0 2.0 %copy-done = bf16[2048,896]{1,0:T(8,128)(2,1)S(1)} copy-done((bf16[2048,896]{1,0:T(8,128)(2,1)S(1)}, bf16[2048,896]{1,0:T(8,128)(2,1)}, u32[]{:S(2)}) %copy-start) | copy-done | bytes 3670040
  91.0 0.0 copy-start.1
  91.0 0.7 copy-done.1
  91.7 0.0 copy-start.2
  91.7 0.7 copy-done.2
  92.4 0.0 copy-start.3
  92.4 0.7 copy-done.3
  93.1 0.0 copy-start.4
  93.1 0.7 copy-done.4
  93.8 0.0 copy-start.5
  93.8 0.7 copy-done.5
  94.4 0.7 copy-done.6
  95.1 0.7 copy-done.7
  95.7 13.9 %shard_map.145 = bf16[512,256]{1,0:T(8,128)(2,1)S(1)} custom-call(f32[2]{0:T(128)S(1)} %copy-done.5, f32[2]{0:T(128)S(1)} %copy-done.6, bf16[128,2048]{1,0:T(8,128)(2,1)S(1)} %all_gather.6.x0_ref, bf16[128,2048]{1,0:T(8,128)(2,1)S(1)} %collective-permute-done.x1_ref, bf16[128,2048]{1,0:T(8,128)(2,1)S(1)} %collective-permute-done.1.x2_ref, ...), custom_call_target="tpu_custom_call" | custom-call | tf_op jit(solution)/shard_map/pallas_call | solution.py:239
  109.6 14.0 %all_to_all.19 = bf16[16,32,256]{2,1,0:T(8,128)(2,1)S(1)} all-to-all(bf16[16,32,256]{2,1,0:T(8,128)(2,1)S(1)} %bitcast.5), channel_id=1, replica_groups=mesh['dp'=32,'tp'=16] {'tp'}, dimensions={0} | all-to-all | bytes 524288 | tf_op jit(solution)/shard_map/all_to_all | solution.py:247
  123.6 0.7 copy.19
  (4 shorter events, 0.0 us)
Async XLA Ops:
  6.5 82.5 %all-gather.2.cloned.1.call-start = ((), (), s32[]{:S(2)}) async-start(), calls=%async_computation.1 | async-start | bytes 3784704 | tf_op jit(solution)/shard_map/all_gather | solution.py:228
  22.9 17.8 %collective-permute-start.2 = (bf16[128,2048]{1,0:T(8,128)(2,1)S(1)}, bf16[128,2048]{1,0:T(8,128)(2,1)S(1)}, u32[]{:S(2)}, u32[]{:S(2)}) collective-permute-start(bf16[128,2048]{1,0:T(8,128)(2,1)S(1)} %all_gather.6.x0_ref), channel_id=1, source_target_pairs={{0,12},{1,13},{2,14},{3,15},{4,0},{5,1},{6,2},{7,3},{8,4},{9,5},{1... | collective-permute-start | bytes 1572872 | tf_op jit(solution)/shard_map/ppermute | solution.py:234
  28.7 12.3 %collective-permute-start.1 = (bf16[128,2048]{1,0:T(8,128)(2,1)S(1)}, bf16[128,2048]{1,0:T(8,128)(2,1)S(1)}, u32[]{:S(2)}, u32[]{:S(2)}) collective-permute-start(bf16[128,2048]{1,0:T(8,128)(2,1)S(1)} %all_gather.6.x0_ref), channel_id=1, source_target_pairs={{0,8},{1,9},{2,10},{3,11},{4,12},{5,13},{6,14},{7,15},{8,0},{9,1},... | collective-permute-start | bytes 1572872 | tf_op jit(solution)/shard_map/ppermute | solution.py:234
  31.1 25.1 %collective-permute-start = (bf16[128,2048]{1,0:T(8,128)(2,1)S(1)}, bf16[128,2048]{1,0:T(8,128)(2,1)S(1)}, u32[]{:S(2)}, u32[]{:S(2)}) collective-permute-start(bf16[128,2048]{1,0:T(8,128)(2,1)S(1)} %all_gather.6.x0_ref), channel_id=1, source_target_pairs={{0,4},{1,5},{2,6},{3,7},{4,8},{5,9},{6,10},{7,11},{8,12},{9,13},{1... | collective-permute-start | bytes 1572872 | tf_op jit(solution)/shard_map/ppermute | solution.py:234
  89.0 2.0 %copy-start = (bf16[2048,896]{1,0:T(8,128)(2,1)S(1)}, bf16[2048,896]{1,0:T(8,128)(2,1)}, u32[]{:S(2)}) copy-start(bf16[2048,896]{1,0:T(8,128)(2,1)} %all-gather.2.cloned.1.call-done.w_ref) | copy-start | bytes 11010052
  91.0 0.7 copy-start.1
  91.7 0.7 copy-start.2
  92.4 0.7 copy-start.3
  93.1 0.7 copy-start.4
  93.8 0.7 copy-start.5
  94.4 0.7 copy-start.6
  95.1 0.7 copy-start.7
Sparse Core Ops, SparseCore 0:
  9.8 79.1 all-gather.1

commit v2 on v1

--- a/solution.py
+++ b/solution.py
@@ -7,6 +7,8 @@
 
 BLOCK = 128
 BASE = 16
+NEAR = (0, 4, 2, 6)
+FAR = (1, 5, 3, 7)
 
 
 def split_two(x):
@@ -18,11 +20,19 @@
 def dot_split(a, b):
     ah, al = split_two(a)
     bh, bl = split_two(b)
-    return jnp.dot(
-        jnp.concatenate([ah, al, ah], axis=1),
-        jnp.concatenate([bh, bh, bl], axis=0),
+    if b.shape[1] > 128:
+        high = jnp.concatenate([bh, bh], axis=0)
+        both = jnp.concatenate([ah, al], axis=1)
+        return jnp.dot(both, high, preferred_element_type=jnp.float32) + jnp.dot(
+            ah, bl, preferred_element_type=jnp.float32
+        )
+    halves = jnp.concatenate([bh, bl], axis=1)
+    both = jnp.dot(
+        jnp.concatenate([ah, al], axis=1),
+        jnp.concatenate([halves, halves], axis=0),
         preferred_element_type=jnp.float32,
     )
+    return both[:, : b.shape[1]] + both[:, b.shape[1] :]
 
 
 def iota(shape, axis):
@@ -57,8 +67,8 @@
 
 
 def mix_kernel(
-    rate_ref, bias_ref, x0_ref, x1_ref, x2_ref, x3_ref, w_ref, seg_ref, tq_ref, tk_ref, tv_ref, gain_ref,
-    out_ref, x_ref, p_ref
+    rate_ref, bias_ref, x0_ref, x1_ref, x2_ref, x3_ref, near_ref, far_ref, other_near_ref, other_far_ref, last_ref,
+    seg_ref, tq_ref, tk_ref, tv_ref, gain_ref, out_ref, x_ref, w_ref, p_ref
 ):
     rows = p_ref.shape[0]
     quarter = rows // 4
@@ -66,6 +76,17 @@
     for ref, behind in ((x0_ref, 0), (x1_ref, 1), (x2_ref, 2), (x3_ref, 3)):
         place = lax.rem(mine + 4 - behind, 4)
         x_ref[pl.ds(pl.multiple_of(place * quarter, quarter), quarter), :] = ref[...]
+    group = lax.axis_index("dp")
+    line = group // 2
+    sign = 2 * lax.rem(group, 2) - 1
+    for ref, offsets, way in (
+        (near_ref, NEAR, sign), (far_ref, FAR, sign), (other_near_ref, NEAR, -sign), (other_far_ref, FAR, -sign), (last_ref, (8,), sign)
+    ):
+        for at, offset in enumerate(offsets):
+            if ref is other_near_ref and offset == 0:
+                continue
+            place = lax.rem(line + 16 + way * offset, 16)
+            w_ref[pl.ds(pl.multiple_of(place * 128, 128), 128), :] = ref[at * 128 : (at + 1) * 128, :]
     p_ref[...] = jnp.dot(x_ref[...], w_ref[...], preferred_element_type=jnp.float32).astype(jnp.bfloat16)
     blocks = rows // BLOCK
     seg_row = seg_ref[...].astype(jnp.float32)
@@ -155,45 +176,54 @@
     spread_columns = jnp.dot(
         jnp.concatenate([high, low], axis=1), picks, preferred_element_type=jnp.float32
     )
-    unit_rows = (iota((BASE, BLOCK), 0) == iota((BASE, BLOCK), 1) % BASE).astype(jnp.float32)
-    inverses = []
-    for i in range(len(problems)):
-        solved = unit_rows
-        for j in range(BASE - 1):
-            factor = spread_columns[i * BASE : (i + 1) * BASE, j * BLOCK : (j + 1) * BLOCK]
-            solved = solved - factor * solved[j : j + 1]
-        inverses.append(solved)
+    count = len(problems)
+    unit_rows = (iota((count, BASE, BLOCK), 1) == iota((count, BASE, BLOCK), 2) % BASE).astype(jnp.float32)
+    solved = unit_rows
+    for j in range(BASE - 1):
+        factor = spread_columns[:, j * BLOCK : (j + 1) * BLOCK].reshape(count, BASE, BLOCK)
+        solved = solved - factor * solved[:, j : j + 1, :]
+
+    inverses = {
+        key_of: jnp.where(base_diagonal, jnp.concatenate([solved[i]] * (BLOCK // BASE), axis=0), 0.0)
+        for i, key_of in enumerate(problems)
+    }
+    size = BASE
+    while size < BLOCK:
+        below = (row_at // (2 * size) == col_at // (2 * size)) & (row_at // size != col_at // size)
+        left = {n: dot_split(inverses[n], jnp.where(below, lowers[n], 0.0)) for n in problems}
+        inverses = {n: inverses[n] - dot_split(left[n], inverses[n]) for n in problems}
+        size = 2 * size
 
     first, state = {}, {}
-    for i, (b, h) in enumerate(problems):
-        span = slice(b * BLOCK, (b + 1) * BLOCK)
-        inverse = jnp.where(base_diagonal, jnp.concatenate([inverses[i]] * (BLOCK // BASE), axis=0), 0.0)
-        size = BASE
-        while size < BLOCK:
-            below = (row_at // (2 * size) == col_at // (2 * size)) & (row_at // size != col_at // size)
-            off = jnp.where(below, lowers[b, h], 0.0)
-            inverse = inverse - dot_split(dot_split(inverse, off), inverse)
-            size = 2 * size
+    for b, h in problems:
+        span = slice(b * BLOCK, (b + 1) * BLOCK)
         right = jnp.concatenate(
             [cols[span, h : h + 1] * values[h][span], cols[span, 8 + h : 9 + h] * key[span]], axis=1
         )
-        solved = dot_split(inverse, right)
-        first[b, h] = solved
+        first[b, h] = dot_split(inverses[b, h], right)
+    for b, h in problems:
+        span = slice(b * BLOCK, (b + 1) * BLOCK)
         if b < blocks - 1:
-            state[b + 1, h] = dot_split((cols[span, 6 + h : 7 + h] * key[span]).T, solved[:, :128])
+            state[b + 1, h] = dot_split((cols[span, 6 + h : 7 + h] * key[span]).T, first[b, h][:, :128])
     gain = gain_ref[...]
-    for b, h in problems:
-        span = slice(b * BLOCK, (b + 1) * BLOCK)
-        update = first[b, h][:, :128]
+    carried = {}
+    for b, h in problems:
+        span = slice(b * BLOCK, (b + 1) * BLOCK)
         if b > 0:
-            both = dot_split(
+            carried[b, h] = dot_split(
                 jnp.concatenate([first[b, h][:, 128:], cols[span, 4 + h : 5 + h] * query[span]], axis=0),
                 state[b, h],
             )
-            update = update - both[:BLOCK]
-            mixed = both[BLOCK:] + dot_split(scores[b, h], update)
+    outs = {}
+    for b, h in problems:
+        update = first[b, h][:, :128]
+        if b > 0:
+            outs[b, h] = carried[b, h][BLOCK:] + dot_split(scores[b, h], update - carried[b, h][:BLOCK])
         else:
-            mixed = dot_split(scores[b, h], update)
+            outs[b, h] = dot_split(scores[b, h], update)
+    for b, h in problems:
+        span = slice(b * BLOCK, (b + 1) * BLOCK)
+        mixed = outs[b, h]
         normed = mixed * lax.rsqrt(jnp.mean(mixed * mixed, axis=-1, keepdims=True) + 1e-06) * gain
         gate = silu(p_ref[span, 512 + 128 * h : 640 + 128 * h].astype(jnp.float32))
         out_ref[span, 128 * h : 128 * (h + 1)] = (normed * gate).astype(jnp.bfloat16)
@@ -225,25 +255,51 @@
     joined = jnp.concatenate(
         [w_query, w_key, w_value, w_gate, w_beta, w_decay, jnp.zeros((w_beta.shape[0], 124), jnp.bfloat16)], axis=1
     )
-    weights = lax.all_gather(joined, "dp", axis=0, tiled=True)
     normed = rms_rows(tokens, norm_gain)
+
+    def along_z(block, shift):
+        up = [(2 * z, 2 * ((z + shift) % 16)) for z in range(16)]
+        down = [(2 * z + 1, 2 * ((z - shift) % 16) + 1) for z in range(16)]
+        return lax.ppermute(block, "dp", up + down)
+
+    def to_other_core(block):
+        return lax.ppermute(block, "dp", [(i, i ^ 1) for i in range(32)])
+
+    def along_x(block, shift):
+        return lax.ppermute(block, "tp", [(i, (i + 4 * shift) % 16) for i in range(16)])
+
+    chips = [[2 * z, 2 * z + 1] for z in range(16)]
     lines = [[4 * x + y for y in range(4)] for x in range(4)]
+    pair = lax.all_gather(joined, "dp", axis=0, tiled=True, axis_index_groups=chips)
+    by_four = along_z(pair, 4)
     quarter = lax.all_gather(normed, "tp", axis=0, tiled=True, axis_index_groups=lines)
-
-    def from_behind(shift):
-        return lax.ppermute(quarter, "tp", [(i, (i + 4 * shift) % 16) for i in range(16)])
-
-    rows = [quarter, from_behind(1), from_behind(2), from_behind(3)]
+    pair, by_four, quarter = lax.optimization_barrier((pair, by_four, quarter))
+    behind, ahead = along_x(quarter, 1), along_x(quarter, 3)
+    two = jnp.concatenate([pair, by_four], axis=0)
+    by_two = along_z(two, 2)
+    near = jnp.concatenate([two, by_two], axis=0)
+    far = along_z(near, 1)
+    last = along_z(by_two[128:], 2)
+    across = along_x(behind, 1)
+    ahead, held = lax.optimization_barrier((ahead, near))
+    other_near = to_other_core(held)
+    far, last, across, other_near = lax.optimization_barrier((far, last, across, other_near))
+    weights = [near, far, other_near, to_other_core(far), last]
+    rows = [quarter, behind, across, ahead]
     vmem = pl.BlockSpec(memory_space=pltpu.VMEM)
     smem = pl.BlockSpec(memory_space=pltpu.SMEM)
     tiles = pl.pallas_call(
         mix_kernel,
         out_shape=jax.ShapeDtypeStruct((512, 256), jnp.bfloat16),
-        in_specs=[smem, smem] + [vmem] * 10,
+        in_specs=[smem, smem] + [vmem] * 14,
         out_specs=vmem,
-        scratch_shapes=[pltpu.VMEM((512, 2048), jnp.bfloat16), pltpu.VMEM((512, 896), jnp.bfloat16)],
+        scratch_shapes=[
+            pltpu.VMEM((512, 2048), jnp.bfloat16),
+            pltpu.VMEM((2048, 896), jnp.bfloat16),
+            pltpu.VMEM((512, 896), jnp.bfloat16),
+        ],
         compiler_params=pltpu.CompilerParams(vmem_limit_bytes=40 * 1024 * 1024),
-    )(decay_rate, dt_bias, *rows, weights, seg_ids, conv_query, conv_key, conv_value, out_gain.reshape(1, 128))
+    )(decay_rate, dt_bias, *rows, *weights, seg_ids, conv_query, conv_key, conv_value, out_gain.reshape(1, 128))
     return lax.all_to_all(tiles, "tp", split_axis=0, concat_axis=1, tiled=True)
 
 

time: 132 us -> 97.3 us (0.74)
  waiting for transfers between devices: 55.4 us -> 16.4 us
  starting transfers between devices: 10.7 us -> 36.9 us
  between operations: 13.4 us -> 0.25 us
  local copies, waits for them, and re-layouts: 10.5 us -> 3.25 us
  blocking collectives: 25.2 us -> 32.1 us
  Pallas kernels: 13.9 us -> 7.38 us
  other arithmetic: 2.06 us -> 0.28 us
    all_gather x1 -> x0, waiting for transfers between devices: 32.8 us -> none  [shards(): weights = lax.all_gather(joined, 'dp', axis=0, tiled=True)]
    ppermute x3 -> x9, starting transfers between devices: 10.7 us -> 36.9 us  [the longest x4 21.4 us: along_z(): return lax.ppermute(block, 'dp', up + down)]
    all_gather x0 -> x1, blocking collectives: none -> 8.62 us  [shards(): lax.all_gather(joined, 'dp', axis=0, tiled=True, axis_index_groups=chips)]
    unnamed x18 -> x28, local copies, waits for them, and re-layouts: 8.25 us -> 1.58 us
    pallas_call x1, Pallas kernels: 13.9 us -> 7.38 us  [shards(): pl.pallas_call(mix_kernel, out_shape=jax.ShapeDtypeStruct((512, 256), jnp...]
    ppermute x3 -> x9, waiting for transfers between devices: 22.5 us -> 16.4 us  [the longest x4 9.2 us: along_z(): return lax.ppermute(block, 'dp', up + down)]
    all_to_all x1, blocking collectives: 14 us -> 12.4 us  [shards(): return lax.all_to_all(tiles, 'tp', split_axis=0, concat_axis=1, tiled=True)]
  transfers between devices with their start and end apart: 4 -> 9, of which waited for: 4 -> 5; matrix products, arithmetic and copies ran while one was open for 2% -> 0% of each run, Pallas kernels for 0% -> 0%
where the time goes in v2:
time: 97.3 us; the launch traced here: 96.5 us
  starting transfers between devices  36.9 us (38%)
  blocking collectives  32.1 us (33%)
  waiting for transfers between devices  16.4 us (17%)
  Pallas kernels  7.38 us (8%)
  local copies, waits for them, and re-layouts  3.25 us (3%)
    ppermute x4, starting transfers between devices, along_z(): return lax.ppermute(block, 'dp', up + down)  21.4 us
    all_to_all x1, blocking collectives, shards(): return lax.all_to_all(tiles, 'tp', split_axis=0, concat_axis=1, tiled=True)  12.4 us
    all_gather x1, blocking collectives, shards(): lax.all_gather(normed, 'tp', axis=0, tiled=True, axis_index_groups=lines)  11.1 us
    ppermute x4, waiting for transfers between devices, along_z(): return lax.ppermute(block, 'dp', up + down)  9.2 us
    all_gather x1, blocking collectives, shards(): lax.all_gather(joined, 'dp', axis=0, tiled=True, axis_index_groups=chips)  8.62 us
    ppermute x3, starting transfers between devices, along_x(): lax.ppermute(block, 'tp', [(i, (i + 4 * shift) % 16) for i in range(16)])  8.21 us
    pallas_call x1, Pallas kernels, shards(): pl.pallas_call(mix_kernel, out_shape=jax.ShapeDtypeStruct((512, 256), jnp...  7.38 us
    ppermute x2, starting transfers between devices, to_other_core(): return lax.ppermute(block, 'dp', [(i, i ^ 1) for i in range(32)])  7.35 us
  transfers between devices with their start and end apart: 9, of which 5 were waited for; matrix products, arithmetic and copies ran while one was open for 0% of the time, Pallas kernels for 0%

profile of v2, /device:TPU:1, one launch (start us, length us, event | category | flops | bytes accessed | tf_op | source)
XLA Modules:
  0.0 96.5 jit_solution(1795487405982916856)
XLA Ops:
  0.0 0.8 copy.16
  0.8 0.1 copy.17
  0.9 0.6 copy-done.9
  1.5 0.9 concatenate.10
  2.4 0.0 copy-start.7
  2.4 8.6 %all_gather.6 = bf16[128,896]{1,0:T(8,128)(2,1)S(1)} all-gather(bf16[64,896]{1,0:T(8,128)(2,1)S(1)} %concatenate.10), channel_id=1, replica_groups={{0,16},{32,48},{64,80},{96,112},{128,144},{160,176},{192,208},{224,240}..., dimensions={0}, use_global_device_ids=true | all-gather | bytes 344064 | tf_op jit(solution)/shard_map/all_gather | solution.py:273
  11.0 7.2 %collective-permute-start = (bf16[128,896]{1,0:T(8,128)(2,1)S(1)}, bf16[128,896]{1,0:T(8,128)(2,1)S(1)}, u32[]{:S(2)}, u32[]{:S(2)}) collective-permute-start(bf16[128,896]{1,0:T(8,128)(2,1)S(1)} %all_gather.6), channel_id=1, source_target_pairs={{0,128},{32,160},{64,192},{96,224},{128,256},{160,288},{192,320},{... | collective-permute-start | bytes 688136 | tf_op jit(solution)/shard_map/ppermute | solution.py:263
  18.2 0.1 fusion
  18.4 0.1 fusion.2
  18.5 11.1 %all_gather.7.x0_ref = bf16[128,2048]{1,0:T(8,128)(2,1)S(1)} all-gather(bf16[32,2048]{1,0:T(8,128)(2,1)S(1)} %fusion.2), channel_id=1, replica_groups={{0,1,2,3},{4,5,6,7},{8,9,10,11},{12,13,14,15},{16,17,18,19},{20,21,22,2..., dimensions={0}, use_global_device_ids=true | all-gather | bytes 655360 | tf_op jit(solution)/shard_map/all_gather | solution.py:275
  29.6 4.6 %collective-permute-start.2 = (bf16[256,896]{1,0:T(8,128)(2,1)S(1)}, bf16[256,896]{1,0:T(8,128)(2,1)S(1)}, u32[]{:S(2)}, u32[]{:S(2)}) collective-permute-start(bf16[256,896]{1,0:T(8,128)(2,1)S(1)} %pad_maximum_fusion), channel_id=1, source_target_pairs={{0,64},{32,96},{64,128},{96,160},{128,192},{160,224},{192,256},{22... | collective-permute-start | bytes 1376264 | tf_op jit(solution)/shard_map/ppermute | solution.py:263
  34.2 4.4 %collective-permute-start.6 = (bf16[128,2048]{1,0:T(8,128)(2,1)S(1)}, bf16[128,2048]{1,0:T(8,128)(2,1)S(1)}, u32[]{:S(2)}, u32[]{:S(2)}) collective-permute-start(bf16[128,2048]{1,0:T(8,128)(2,1)S(1)} %all_gather.7.x0_ref), channel_id=1, source_target_pairs={{0,12},{1,13},{2,14},{3,15},{4,0},{5,1},{6,2},{7,3},{8,4},{9,5},{1... | collective-permute-start | bytes 1572872 | tf_op jit(solution)/shard_map/ppermute | solution.py:269
  38.6 1.9 %collective-permute-start.1 = (bf16[128,2048]{1,0:T(8,128)(2,1)S(1)}, bf16[128,2048]{1,0:T(8,128)(2,1)S(1)}, u32[]{:S(2)}, u32[]{:S(2)}) collective-permute-start(bf16[128,2048]{1,0:T(8,128)(2,1)S(1)} %all_gather.7.x0_ref), channel_id=1, source_target_pairs={{0,4},{1,5},{2,6},{3,7},{4,8},{5,9},{6,10},{7,11},{8,12},{9,13},{1... | collective-permute-start | bytes 1572872 | tf_op jit(solution)/shard_map/ppermute | solution.py:269
  40.6 4.2 %collective-permute-done.2 = bf16[256,896]{1,0:T(8,128)(2,1)S(1)} collective-permute-done((bf16[256,896]{1,0:T(8,128)(2,1)S(1)}, bf16[256,896]{1,0:T(8,128)(2,1)S(1)}, u32[]{:S(2)}, u32[]{:S(2)}) %collective-permute-start.2) | collective-permute-done | bytes 458784 | tf_op jit(solution)/shard_map/ppermute | solution.py:263
  44.8 4.7 %collective-permute-start.3 = (bf16[512,896]{1,0:T(8,128)(2,1)S(1)}, bf16[512,896]{1,0:T(8,128)(2,1)S(1)}, u32[]{:S(2)}, u32[]{:S(2)}) collective-permute-start(bf16[512,896]{1,0:T(8,128)(2,1)S(1)} %constant_dynamic-update-slice_fusion.near_ref), channel_id=1, source_target_pairs={{0,32},{32,64},{64,96},{96,128},{128,160},{160,192},{192,224},{224... | collective-permute-start | bytes 2752520 | tf_op jit(solution)/shard_map/ppermute | solution.py:263
  49.6 0.0 collective-permute-done.6.x3_ref
  49.6 3.1 %collective-permute-start.7 = (bf16[512,896]{1,0:T(8,128)(2,1)S(1)}, bf16[512,896]{1,0:T(8,128)(2,1)S(1)}, u32[]{:S(2)}, u32[]{:S(2)}) collective-permute-start(bf16[512,896]{1,0:T(8,128)(2,1)S(1)} %constant_dynamic-update-slice_fusion.near_ref), channel_id=1, source_target_pairs={{0,16},{16,0},{32,48},{48,32},{64,80},{80,64},{96,112},{112,96},{1... | collective-permute-start | bytes 2752520 | tf_op jit(solution)/shard_map/ppermute | solution.py:266
  52.6 1.9 %collective-permute-done.1.x1_ref = bf16[128,2048]{1,0:T(8,128)(2,1)S(1)} collective-permute-done((bf16[128,2048]{1,0:T(8,128)(2,1)S(1)}, bf16[128,2048]{1,0:T(8,128)(2,1)S(1)}, u32[]{:S(2)}, u32[]{:S(2)}) %collective-permute-start.1) | collective-permute-done | bytes 524320 | tf_op jit(solution)/shard_map/ppermute | solution.py:269
  54.6 1.9 %collective-permute-start.5 = (bf16[128,2048]{1,0:T(8,128)(2,1)S(1)}, bf16[128,2048]{1,0:T(8,128)(2,1)S(1)}, u32[]{:S(2)}, u32[]{:S(2)}) collective-permute-start(bf16[128,2048]{1,0:T(8,128)(2,1)S(1)} %collective-permute-done.1.x1_ref), channel_id=1, source_target_pairs={{0,4},{1,5},{2,6},{3,7},{4,8},{5,9},{6,10},{7,11},{8,12},{9,13},{1... | collective-permute-start | bytes 1572872 | tf_op jit(solution)/shard_map/ppermute | solution.py:269
  56.5 0.0 copy-start
  56.5 0.0 copy-start.1
  56.6 0.0 copy-start.3
  56.6 0.0 copy-start.4
  56.6 0.0 copy-start.5
  56.6 4.8 %collective-permute-start.4 = (bf16[128,896]{1,0:T(8,128)(2,1)S(1)}, bf16[128,896]{1,0:T(8,128)(2,1)S(1)}, u32[]{:S(2)}, u32[]{:S(2)}) collective-permute-start(bf16[128,896]{1,0:T(8,128)(2,1)S(1)} %slice.4), channel_id=1, source_target_pairs={{0,64},{32,96},{64,128},{96,160},{128,192},{160,224},{192,256},{22... | collective-permute-start | bytes 688136 | tf_op jit(solution)/shard_map/ppermute | solution.py:263
  61.5 5.0 %collective-permute-done.4.last_ref = bf16[128,896]{1,0:T(8,128)(2,1)S(1)} collective-permute-done((bf16[128,896]{1,0:T(8,128)(2,1)S(1)}, bf16[128,896]{1,0:T(8,128)(2,1)S(1)}, u32[]{:S(2)}, u32[]{:S(2)}) %collective-permute-start.4) | collective-permute-done | bytes 229408 | tf_op jit(solution)/shard_map/ppermute | solution.py:263
  66.5 3.1 %collective-permute-done.5.x2_ref = bf16[128,2048]{1,0:T(8,128)(2,1)S(1)} collective-permute-done((bf16[128,2048]{1,0:T(8,128)(2,1)S(1)}, bf16[128,2048]{1,0:T(8,128)(2,1)S(1)}, u32[]{:S(2)}, u32[]{:S(2)}) %collective-permute-start.5) | collective-permute-done | bytes 524320 | tf_op jit(solution)/shard_map/ppermute | solution.py:269
  69.6 4.3 %collective-permute-start.8 = (bf16[512,896]{1,0:T(8,128)(2,1)S(1)}, bf16[512,896]{1,0:T(8,128)(2,1)S(1)}, u32[]{:S(2)}, u32[]{:S(2)}) collective-permute-start(bf16[512,896]{1,0:T(8,128)(2,1)S(1)} %collective-permute-done.3.far_ref), channel_id=1, source_target_pairs={{0,16},{16,0},{32,48},{48,32},{64,80},{80,64},{96,112},{112,96},{1... | collective-permute-start | bytes 2752520 | tf_op jit(solution)/shard_map/ppermute | solution.py:266
  73.9 2.1 %collective-permute-done.8.other_far_ref = bf16[512,896]{1,0:T(8,128)(2,1)S(1)} collective-permute-done((bf16[512,896]{1,0:T(8,128)(2,1)S(1)}, bf16[512,896]{1,0:T(8,128)(2,1)S(1)}, u32[]{:S(2)}, u32[]{:S(2)}) %collective-permute-start.8) | collective-permute-done | bytes 917536 | tf_op jit(solution)/shard_map/ppermute | solution.py:266
  76.1 7.4 %shard_map.145 = bf16[512,256]{1,0:T(8,128)(2,1)S(1)} custom-call(f32[2]{0:T(128)S(1)} %copy-done.4, f32[2]{0:T(128)S(1)} %copy-done.5, bf16[128,2048]{1,0:T(8,128)(2,1)S(1)} %all_gather.7.x0_ref, bf16[128,2048]{1,0:T(8,128)(2,1)S(1)} %collective-permute-done.1.x1_ref, bf16[128,2048]{1,0:T(8,128)(2,1)S(1)} %collective-permute-done.5.x2_ref, ...), custom_call_target="tpu_custom_call" | custom-call | tf_op jit(solution)/shard_map/pallas_call | solution.py:291
  83.5 12.4 %all_to_all.19 = bf16[16,32,256]{2,1,0:T(8,128)(2,1)S(1)} all-to-all(bf16[16,32,256]{2,1,0:T(8,128)(2,1)S(1)} %bitcast.5), channel_id=1, replica_groups=mesh['dp'=32,'tp'=16] {'tp'}, dimensions={0} | all-to-all | bytes 524288 | tf_op jit(solution)/shard_map/all_to_all | solution.py:303
  95.8 0.7 copy.19
  (27 shorter events, 0.2 us)
Async XLA Ops:
  0.0 0.8 copy-start.11
  0.0 0.9 copy-start.8
  0.8 0.7 copy-start.9
  2.4 15.8 %copy-start.7 = (bf16[32,2048]{1,0:T(8,128)(2,1)S(1)}, bf16[32,2048]{1,0:T(8,128)(2,1)}, u32[]{:S(2)}) copy-start(bf16[32,2048]{1,0:T(8,128)(2,1)} %param.15) | copy-start | bytes 393220
  11.0 7.4 %copy-start.10 = (f32[2048]{0:T(1024)S(1)}, f32[2048]{0:T(1024)}, u32[]{:S(2)}) copy-start(f32[2048]{0:T(1024)} %param.16) | copy-start | bytes 24580
  11.0 18.6 %collective-permute-start = (bf16[128,896]{1,0:T(8,128)(2,1)S(1)}, bf16[128,896]{1,0:T(8,128)(2,1)S(1)}, u32[]{:S(2)}, u32[]{:S(2)}) collective-permute-start(bf16[128,896]{1,0:T(8,128)(2,1)S(1)} %all_gather.6), channel_id=1, source_target_pairs={{0,128},{32,160},{64,192},{96,224},{128,256},{160,288},{192,320},{... | collective-permute-start | bytes 688136 | tf_op jit(solution)/shard_map/ppermute | solution.py:263
  29.6 15.1 %collective-permute-start.2 = (bf16[256,896]{1,0:T(8,128)(2,1)S(1)}, bf16[256,896]{1,0:T(8,128)(2,1)S(1)}, u32[]{:S(2)}, u32[]{:S(2)}) collective-permute-start(bf16[256,896]{1,0:T(8,128)(2,1)S(1)} %pad_maximum_fusion), channel_id=1, source_target_pairs={{0,64},{32,96},{64,128},{96,160},{128,192},{160,224},{192,256},{22... | collective-permute-start | bytes 1376264 | tf_op jit(solution)/shard_map/ppermute | solution.py:263
  34.2 15.3 %collective-permute-start.6 = (bf16[128,2048]{1,0:T(8,128)(2,1)S(1)}, bf16[128,2048]{1,0:T(8,128)(2,1)S(1)}, u32[]{:S(2)}, u32[]{:S(2)}) collective-permute-start(bf16[128,2048]{1,0:T(8,128)(2,1)S(1)} %all_gather.7.x0_ref), channel_id=1, source_target_pairs={{0,12},{1,13},{2,14},{3,15},{4,0},{5,1},{6,2},{7,3},{8,4},{9,5},{1... | collective-permute-start | bytes 1572872 | tf_op jit(solution)/shard_map/ppermute | solution.py:269
  38.6 16.0 %collective-permute-start.1 = (bf16[128,2048]{1,0:T(8,128)(2,1)S(1)}, bf16[128,2048]{1,0:T(8,128)(2,1)S(1)}, u32[]{:S(2)}, u32[]{:S(2)}) collective-permute-start(bf16[128,2048]{1,0:T(8,128)(2,1)S(1)} %all_gather.7.x0_ref), channel_id=1, source_target_pairs={{0,4},{1,5},{2,6},{3,7},{4,8},{5,9},{6,10},{7,11},{8,12},{9,13},{1... | collective-permute-start | bytes 1572872 | tf_op jit(solution)/shard_map/ppermute | solution.py:269
  44.8 24.8 %collective-permute-start.3 = (bf16[512,896]{1,0:T(8,128)(2,1)S(1)}, bf16[512,896]{1,0:T(8,128)(2,1)S(1)}, u32[]{:S(2)}, u32[]{:S(2)}) collective-permute-start(bf16[512,896]{1,0:T(8,128)(2,1)S(1)} %constant_dynamic-update-slice_fusion.near_ref), channel_id=1, source_target_pairs={{0,32},{32,64},{64,96},{96,128},{128,160},{160,192},{192,224},{224... | collective-permute-start | bytes 2752520 | tf_op jit(solution)/shard_map/ppermute | solution.py:263
  49.6 20.0 %collective-permute-start.7 = (bf16[512,896]{1,0:T(8,128)(2,1)S(1)}, bf16[512,896]{1,0:T(8,128)(2,1)S(1)}, u32[]{:S(2)}, u32[]{:S(2)}) collective-permute-start(bf16[512,896]{1,0:T(8,128)(2,1)S(1)} %constant_dynamic-update-slice_fusion.near_ref), channel_id=1, source_target_pairs={{0,16},{16,0},{32,48},{48,32},{64,80},{80,64},{96,112},{112,96},{1... | collective-permute-start | bytes 2752520 | tf_op jit(solution)/shard_map/ppermute | solution.py:266
  54.6 15.0 %collective-permute-start.5 = (bf16[128,2048]{1,0:T(8,128)(2,1)S(1)}, bf16[128,2048]{1,0:T(8,128)(2,1)S(1)}, u32[]{:S(2)}, u32[]{:S(2)}) collective-permute-start(bf16[128,2048]{1,0:T(8,128)(2,1)S(1)} %collective-permute-done.1.x1_ref), channel_id=1, source_target_pairs={{0,4},{1,5},{2,6},{3,7},{4,8},{5,9},{6,10},{7,11},{8,12},{9,13},{1... | collective-permute-start | bytes 1572872 | tf_op jit(solution)/shard_map/ppermute | solution.py:269
  56.5 19.5 %copy-start = (f32[4,256]{1,0:T(4,128)S(1)}, f32[4,256]{1,0:T(4,128)}, u32[]{:S(2)}) copy-start(f32[4,256]{1,0:T(4,128)} %tv_ref.1) | copy-start | bytes 12292
  56.5 19.5 %copy-start.1 = (s32[1,512]{1,0:T(1,128)S(1)}, s32[1,512]{1,0:T(1,128)}, u32[]{:S(2)}) copy-start(s32[1,512]{1,0:T(1,128)} %seg_ref.1) | copy-start | bytes 6148
  56.5 19.5 %copy-start.2 = (f32[4,128]{1,0:T(4,128)S(1)}, f32[4,128]{1,0:T(4,128)}, u32[]{:S(2)}) copy-start(f32[4,128]{1,0:T(4,128)} %tq_ref.1) | copy-start | bytes 6148
  56.6 19.5 %copy-start.3 = (f32[4,128]{1,0:T(4,128)S(1)}, f32[4,128]{1,0:T(4,128)}, u32[]{:S(2)}) copy-start(f32[4,128]{1,0:T(4,128)} %tk_ref.1) | copy-start | bytes 6148
  56.6 19.4 %copy-start.4 = (f32[2]{0:T(128)S(1)}, f32[2]{0:T(128)}, u32[]{:S(2)}) copy-start(f32[2]{0:T(128)} %rate_ref.1) | copy-start | bytes 28
  56.6 19.4 %copy-start.5 = (f32[2]{0:T(128)S(1)}, f32[2]{0:T(128)}, u32[]{:S(2)}) copy-start(f32[2]{0:T(128)} %bias_ref.1) | copy-start | bytes 28
  56.6 19.4 %copy-start.6 = (f32[128]{0:T(128)S(1)}, f32[128]{0:T(128)}, u32[]{:S(2)}) copy-start(f32[128]{0:T(128)} %param.28) | copy-start | bytes 1540
  56.6 9.9 %collective-permute-start.4 = (bf16[128,896]{1,0:T(8,128)(2,1)S(1)}, bf16[128,896]{1,0:T(8,128)(2,1)S(1)}, u32[]{:S(2)}, u32[]{:S(2)}) collective-permute-start(bf16[128,896]{1,0:T(8,128)(2,1)S(1)} %slice.4), channel_id=1, source_target_pairs={{0,64},{32,96},{64,128},{96,160},{128,192},{160,224},{192,256},{22... | collective-permute-start | bytes 688136 | tf_op jit(solution)/shard_map/ppermute | solution.py:263
  69.6 6.4 %collective-permute-start.8 = (bf16[512,896]{1,0:T(8,128)(2,1)S(1)}, bf16[512,896]{1,0:T(8,128)(2,1)S(1)}, u32[]{:S(2)}, u32[]{:S(2)}) collective-permute-start(bf16[512,896]{1,0:T(8,128)(2,1)S(1)} %collective-permute-done.3.far_ref), channel_id=1, source_target_pairs={{0,16},{16,0},{32,48},{48,32},{64,80},{80,64},{96,112},{112,96},{1... | collective-permute-start | bytes 2752520 | tf_op jit(solution)/shard_map/ppermute | solution.py:266

commit v3 on v2

--- a/solution.py
+++ b/solution.py
@@ -66,12 +66,36 @@
     return x * lax.rsqrt(jnp.sum(x * x, axis=-1, keepdims=True) + 1e-06)
 
 
-def mix_kernel(
-    rate_ref, bias_ref, x0_ref, x1_ref, x2_ref, x3_ref, near_ref, far_ref, other_near_ref, other_far_ref, last_ref,
-    seg_ref, tq_ref, tk_ref, tv_ref, gain_ref, out_ref, x_ref, w_ref, p_ref
+def pack_kernel(
+    tokens_hbm, norm_hbm, query_hbm, key_hbm, value_hbm, gate_hbm, beta_ref, decay_ref, joined_ref, normed_ref,
+    tokens_ref, norm_ref, sems
 ):
-    rows = p_ref.shape[0]
-    quarter = rows // 4
+    moves = (
+        (tokens_hbm, tokens_ref),
+        (norm_hbm, norm_ref),
+        (query_hbm, joined_ref.at[:, 0:128]),
+        (key_hbm, joined_ref.at[:, 128:256]),
+        (value_hbm, joined_ref.at[:, 256:512]),
+        (gate_hbm, joined_ref.at[:, 512:768]),
+    )
+    copies = [pltpu.make_async_copy(source, target, sems.at[i]) for i, (source, target) in enumerate(moves)]
+    for copy in copies:
+        copy.start()
+    for copy in copies:
+        copy.wait()
+    narrow = jnp.concatenate([beta_ref[...], decay_ref[...]], axis=0).astype(jnp.float32)
+    narrow = jnp.concatenate([narrow, jnp.zeros((4, 64), jnp.float32)], axis=1)
+    narrow = jnp.concatenate([narrow, jnp.zeros((124, 128), jnp.float32)], axis=0).T
+    joined_ref[:, 768:896] = narrow[:64].astype(jnp.bfloat16)
+    floats = tokens_ref[...].astype(jnp.float32)
+    scaled = floats * lax.rsqrt(jnp.mean(floats * floats, axis=-1, keepdims=True) + 1e-06)
+    normed_ref[...] = (scaled * norm_ref[...]).astype(jnp.bfloat16)
+
+
+def project_kernel(
+    x0_ref, x1_ref, x2_ref, x3_ref, near_ref, far_ref, other_near_ref, last_ref, sum_ref, left_ref, x_ref, part_ref
+):
+    quarter = x0_ref.shape[0]
     mine = lax.axis_index("tp") // 4
     for ref, behind in ((x0_ref, 0), (x1_ref, 1), (x2_ref, 2), (x3_ref, 3)):
         place = lax.rem(mine + 4 - behind, 4)
@@ -79,15 +103,29 @@
     group = lax.axis_index("dp")
     line = group // 2
     sign = 2 * lax.rem(group, 2) - 1
-    for ref, offsets, way in (
-        (near_ref, NEAR, sign), (far_ref, FAR, sign), (other_near_ref, NEAR, -sign), (other_far_ref, FAR, -sign), (last_ref, (8,), sign)
-    ):
-        for at, offset in enumerate(offsets):
-            if ref is other_near_ref and offset == 0:
-                continue
-            place = lax.rem(line + 16 + way * offset, 16)
-            w_ref[pl.ds(pl.multiple_of(place * 128, 128), 128), :] = ref[at * 128 : (at + 1) * 128, :]
-    p_ref[...] = jnp.dot(x_ref[...], w_ref[...], preferred_element_type=jnp.float32).astype(jnp.bfloat16)
+
+    def columns(offset):
+        place = lax.rem(line + 16 + offset, 16)
+        return x_ref[:, pl.ds(pl.multiple_of(place * 128, 128), 128)]
+
+    offsets = [sign * n for n in NEAR + FAR] + [-sign * n for n in NEAR[1:]] + [8]
+    for at, offset in enumerate(offsets):
+        part_ref[:, at * 128 : (at + 1) * 128] = columns(offset)
+    for at, n in enumerate(FAR):
+        left_ref[:, at * 128 : (at + 1) * 128] = columns(-sign * n)
+    total = jnp.dot(part_ref[:, 0:512], near_ref[...], preferred_element_type=jnp.float32)
+    total = total + jnp.dot(part_ref[:, 512:1024], far_ref[...], preferred_element_type=jnp.float32)
+    rest = jnp.concatenate([other_near_ref[128:, :], last_ref[...]], axis=0)
+    sum_ref[...] = total + jnp.dot(part_ref[:, 1024:1536], rest, preferred_element_type=jnp.float32)
+
+
+def mix_kernel(
+    rate_ref, bias_ref, sum_ref, left_ref, other_far_ref, seg_ref, tq_ref, tk_ref, tv_ref, gain_ref, out_ref, p_ref
+):
+    rows = p_ref.shape[0]
+    p_ref[...] = (
+        sum_ref[...] + jnp.dot(left_ref[...], other_far_ref[...], preferred_element_type=jnp.float32)
+    ).astype(jnp.bfloat16)
     blocks = rows // BLOCK
     seg_row = seg_ref[...].astype(jnp.float32)
     position = iota((1, rows), 1)
@@ -229,12 +267,6 @@
         out_ref[span, 128 * h : 128 * (h + 1)] = (normed * gate).astype(jnp.bfloat16)
 
 
-def rms_rows(tokens, gain):
-    floats = tokens.astype(jnp.float32)
-    scaled = floats * lax.rsqrt(jnp.mean(floats * floats, axis=-1, keepdims=True) + 1e-06)
-    return (scaled * gain).astype(jnp.bfloat16)
-
-
 def shards(
     tokens,
     norm_gain,
@@ -252,10 +284,24 @@
     out_gain,
     seg_ids,
 ):
-    joined = jnp.concatenate(
-        [w_query, w_key, w_value, w_gate, w_beta, w_decay, jnp.zeros((w_beta.shape[0], 124), jnp.bfloat16)], axis=1
-    )
-    normed = rms_rows(tokens, norm_gain)
+    vmem = pl.BlockSpec(memory_space=pltpu.VMEM)
+    smem = pl.BlockSpec(memory_space=pltpu.SMEM)
+    params = pltpu.CompilerParams(vmem_limit_bytes=40 * 1024 * 1024)
+    joined, normed = pl.pallas_call(
+        pack_kernel,
+        out_shape=(
+            jax.ShapeDtypeStruct((64, 896), jnp.bfloat16),
+            jax.ShapeDtypeStruct(tokens.shape, jnp.bfloat16),
+        ),
+        in_specs=[pl.BlockSpec(memory_space=pl.ANY)] * 6 + [vmem] * 2,
+        out_specs=(vmem, vmem),
+        scratch_shapes=[
+            pltpu.VMEM(tokens.shape, jnp.bfloat16),
+            pltpu.VMEM((1, tokens.shape[1]), jnp.float32),
+            pltpu.SemaphoreType.DMA((6,)),
+        ],
+        compiler_params=pltpu.CompilerParams(vmem_limit_bytes=58 * 1024 * 1024),
+    )(tokens, norm_gain.reshape(1, -1), w_query, w_key, w_value, w_gate, w_beta.T, w_decay.T)
 
     def along_z(block, shift):
         up = [(2 * z, 2 * ((z + shift) % 16)) for z in range(16)]
@@ -280,26 +326,31 @@
     near = jnp.concatenate([two, by_two], axis=0)
     far = along_z(near, 1)
     last = along_z(by_two[128:], 2)
-    across = along_x(behind, 1)
-    ahead, held = lax.optimization_barrier((ahead, near))
+    across = along_x(ahead, 3)
+    behind, held = lax.optimization_barrier((behind, near))
     other_near = to_other_core(held)
     far, last, across, other_near = lax.optimization_barrier((far, last, across, other_near))
-    weights = [near, far, other_near, to_other_core(far), last]
-    rows = [quarter, behind, across, ahead]
-    vmem = pl.BlockSpec(memory_space=pltpu.VMEM)
-    smem = pl.BlockSpec(memory_space=pltpu.SMEM)
+    other_far = to_other_core(far)
+    partial, left = pl.pallas_call(
+        project_kernel,
+        out_shape=(
+            jax.ShapeDtypeStruct((512, 896), jnp.float32),
+            jax.ShapeDtypeStruct((512, 512), jnp.bfloat16),
+        ),
+        in_specs=[vmem] * 8,
+        out_specs=(vmem, vmem),
+        scratch_shapes=[pltpu.VMEM((512, 2048), jnp.bfloat16), pltpu.VMEM((512, 1536), jnp.bfloat16)],
+        compiler_params=params,
+        cost_estimate=pl.CostEstimate(flops=2 * 512 * 1536 * 896, bytes_accessed=8 << 20, transcendentals=0),
+    )(quarter, behind, across, ahead, near, far, other_near, last)
     tiles = pl.pallas_call(
         mix_kernel,
         out_shape=jax.ShapeDtypeStruct((512, 256), jnp.bfloat16),
-        in_specs=[smem, smem] + [vmem] * 14,
+        in_specs=[smem, smem] + [vmem] * 8,
         out_specs=vmem,
-        scratch_shapes=[
-            pltpu.VMEM((512, 2048), jnp.bfloat16),
-            pltpu.VMEM((2048, 896), jnp.bfloat16),
-            pltpu.VMEM((512, 896), jnp.bfloat16),
-        ],
-        compiler_params=pltpu.CompilerParams(vmem_limit_bytes=40 * 1024 * 1024),
-    )(decay_rate, dt_bias, *rows, *weights, seg_ids, conv_query, conv_key, conv_value, out_gain.reshape(1, 128))
+        scratch_shapes=[pltpu.VMEM((512, 896), jnp.bfloat16)],
+        compiler_params=params,
+    )(decay_rate, dt_bias, partial, left, other_far, seg_ids, conv_query, conv_key, conv_value, out_gain.reshape(1, 128))
     return lax.all_to_all(tiles, "tp", split_axis=0, concat_axis=1, tiled=True)
 
 

time: 97.3 us -> 95 us (0.976)
  waiting for transfers between devices: 16.4 us -> 11.9 us
  Pallas kernels: 7.38 us -> 9.96 us
  local copies, waits for them, and re-layouts: 3.25 us -> 0.88 us
  blocking collectives: 32.1 us -> 33.6 us
  starting transfers between devices: 36.9 us -> 37.9 us
    pallas_call x0 -> x2, Pallas kernels: none -> 4.58 us  [the longest x1 2.45 us: shards(): pl.pallas_call(pack_kernel, out_shape=(jax.ShapeDtypeStruct((64, 896), jn...]
    ppermute x3, waiting for transfers between devices: 5.08 us -> 2.44 us  [along_x(): lax.ppermute(block, 'tp', [(i, (i + 4 * shift) % 16) for i in range(16)])]
    ppermute x2, waiting for transfers between devices: 2.08 us -> 0.01 us  [to_other_core(): return lax.ppermute(block, 'dp', [(i, i ^ 1) for i in range(32)])]
    pallas_call x1, Pallas kernels: 7.38 us -> 5.39 us  [shards(): pl.pallas_call(mix_kernel, out_shape=jax.ShapeDtypeStruct((512, 256), jnp...]
    ppermute x3, starting transfers between devices: 8.21 us -> 9.79 us  [along_x(): lax.ppermute(block, 'tp', [(i, (i + 4 * shift) % 16) for i in range(16)])]
    unnamed x28 -> x16, local copies, waits for them, and re-layouts: 1.58 us -> 0.09 us
    all_to_all x1, blocking collectives: 12.4 us -> 13.6 us  [shards(): return lax.all_to_all(tiles, 'tp', split_axis=0, concat_axis=1, tiled=True)]
  transfers between devices with their start and end apart: 9 -> 9, of which waited for: 5 -> 4; matrix products, arithmetic and copies ran while one was open for 0% -> 0% of each run, Pallas kernels for 0% -> 2%
where the time goes in v3:
time: 95 us; the launch traced here: 94.6 us
  starting transfers between devices  37.9 us (40%)
  blocking collectives  33.6 us (35%)
  waiting for transfers between devices  11.9 us (13%)
  Pallas kernels  9.96 us (10%)
    ppermute x4, starting transfers between devices, along_z(): return lax.ppermute(block, 'dp', up + down)  21.5 us
    all_to_all x1, blocking collectives, shards(): return lax.all_to_all(tiles, 'tp', split_axis=0, concat_axis=1, tiled=True)  13.6 us
    all_gather x1, blocking collectives, shards(): lax.all_gather(normed, 'tp', axis=0, tiled=True, axis_index_groups=lines)  11.3 us
    ppermute x3, starting transfers between devices, along_x(): lax.ppermute(block, 'tp', [(i, (i + 4 * shift) % 16) for i in range(16)])  9.79 us
    ppermute x4, waiting for transfers between devices, along_z(): return lax.ppermute(block, 'dp', up + down)  9.5 us
    all_gather x1, blocking collectives, shards(): lax.all_gather(joined, 'dp', axis=0, tiled=True, axis_index_groups=chips)  8.7 us
    ppermute x2, starting transfers between devices, to_other_core(): return lax.ppermute(block, 'dp', [(i, i ^ 1) for i in range(32)])  6.58 us
    pallas_call x1, Pallas kernels, shards(): pl.pallas_call(mix_kernel, out_shape=jax.ShapeDtypeStruct((512, 256), jnp...  5.39 us
  transfers between devices with their start and end apart: 9, of which 4 were waited for; matrix products, arithmetic and copies ran while one was open for 0% of the time, Pallas kernels for 2%

profile of v3, /device:TPU:1, one launch (start us, length us, event | category | flops | bytes accessed | tf_op | source)
XLA Modules:
  0.0 94.6 jit_solution(13148066707922385844)
XLA Ops:
  0.0 2.5 %shard_map.145 = (bf16[64,896]{1,0:T(8,128)(2,1)}, bf16[32,2048]{1,0:T(8,128)(2,1)}) custom-call(bf16[32,2048]{1,0:T(8,128)(2,1)} %tokens_hbm.1, f32[1,2048]{1,0:T(1,128)} %bitcast.11, bf16[64,128]{1,0:T(8,128)(2,1)} %query_hbm.1, bf16[64,128]{1,0:T(8,128)(2,1)} %key_hbm.1, bf16[64,256]{1,0:T(8,128)(2,1)} %value_hbm.1, bf16[64,256]{1,0:T(8,128)(2,1)} %gate_hbm.1, ...), custom_call_target="tpu_custom_call" | custom-call | tf_op jit(solution)/shard_map/pallas_call | solution.py:290
  2.5 8.7 %all_gather.6 = bf16[128,896]{1,0:T(8,128)(2,1)S(1)} all-gather(bf16[64,896]{1,0:T(8,128)(2,1)} %get-tuple-element.18), channel_id=1, replica_groups={{0,16},{32,48},{64,80},{96,112},{128,144},{160,176},{192,208},{224,240}..., dimensions={0}, use_global_device_ids=true | all-gather | bytes 344064 | tf_op jit(solution)/shard_map/all_gather | solution.py:319
  11.2 7.1 %collective-permute-start = (bf16[128,896]{1,0:T(8,128)(2,1)S(1)}, bf16[128,896]{1,0:T(8,128)(2,1)S(1)}, u32[]{:S(2)}, u32[]{:S(2)}) collective-permute-start(bf16[128,896]{1,0:T(8,128)(2,1)S(1)} %all_gather.6), channel_id=1, source_target_pairs={{0,128},{32,160},{64,192},{96,224},{128,256},{160,288},{192,320},{... | collective-permute-start | bytes 688136 | tf_op jit(solution)/shard_map/ppermute | solution.py:309
  18.2 11.3 %all_gather.7.x0_ref = bf16[128,2048]{1,0:T(8,128)(2,1)S(1)} all-gather(bf16[32,2048]{1,0:T(8,128)(2,1)} %get-tuple-element.19), channel_id=1, replica_groups={{0,1,2,3},{4,5,6,7},{8,9,10,11},{12,13,14,15},{16,17,18,19},{20,21,22,2..., dimensions={0}, use_global_device_ids=true | all-gather | bytes 655360 | tf_op jit(solution)/shard_map/all_gather | solution.py:321
  29.6 0.0 collective-permute-done
  29.6 4.7 %collective-permute-start.2 = (bf16[256,896]{1,0:T(8,128)(2,1)S(1)}, bf16[256,896]{1,0:T(8,128)(2,1)S(1)}, u32[]{:S(2)}, u32[]{:S(2)}) collective-permute-start(bf16[256,896]{1,0:T(8,128)(2,1)S(1)} %pad_maximum_fusion), channel_id=1, source_target_pairs={{0,64},{32,96},{64,128},{96,160},{128,192},{160,224},{192,256},{22... | collective-permute-start | bytes 1376264 | tf_op jit(solution)/shard_map/ppermute | solution.py:309
  34.3 3.1 %collective-permute-start.1 = (bf16[128,2048]{1,0:T(8,128)(2,1)S(1)}, bf16[128,2048]{1,0:T(8,128)(2,1)S(1)}, u32[]{:S(2)}, u32[]{:S(2)}) collective-permute-start(bf16[128,2048]{1,0:T(8,128)(2,1)S(1)} %all_gather.7.x0_ref), channel_id=1, source_target_pairs={{0,4},{1,5},{2,6},{3,7},{4,8},{5,9},{6,10},{7,11},{8,12},{9,13},{1... | collective-permute-start | bytes 1572872 | tf_op jit(solution)/shard_map/ppermute | solution.py:315
  37.3 3.4 %collective-permute-start.5 = (bf16[128,2048]{1,0:T(8,128)(2,1)S(1)}, bf16[128,2048]{1,0:T(8,128)(2,1)S(1)}, u32[]{:S(2)}, u32[]{:S(2)}) collective-permute-start(bf16[128,2048]{1,0:T(8,128)(2,1)S(1)} %all_gather.7.x0_ref), channel_id=1, source_target_pairs={{0,12},{1,13},{2,14},{3,15},{4,0},{5,1},{6,2},{7,3},{8,4},{9,5},{1... | collective-permute-start | bytes 1572872 | tf_op jit(solution)/shard_map/ppermute | solution.py:315
  40.8 4.1 %collective-permute-done.2 = bf16[256,896]{1,0:T(8,128)(2,1)S(1)} collective-permute-done((bf16[256,896]{1,0:T(8,128)(2,1)S(1)}, bf16[256,896]{1,0:T(8,128)(2,1)S(1)}, u32[]{:S(2)}, u32[]{:S(2)}) %collective-permute-start.2) | collective-permute-done | bytes 458784 | tf_op jit(solution)/shard_map/ppermute | solution.py:309
  45.0 4.5 %collective-permute-start.3 = (bf16[512,896]{1,0:T(8,128)(2,1)S(1)}, bf16[512,896]{1,0:T(8,128)(2,1)S(1)}, u32[]{:S(2)}, u32[]{:S(2)}) collective-permute-start(bf16[512,896]{1,0:T(8,128)(2,1)S(1)} %constant_dynamic-update-slice_fusion.near_ref), channel_id=1, source_target_pairs={{0,32},{32,64},{64,96},{96,128},{128,160},{160,192},{192,224},{224... | collective-permute-start | bytes 2752520 | tf_op jit(solution)/shard_map/ppermute | solution.py:309
  49.5 1.1 %collective-permute-done.1.x1_ref = bf16[128,2048]{1,0:T(8,128)(2,1)S(1)} collective-permute-done((bf16[128,2048]{1,0:T(8,128)(2,1)S(1)}, bf16[128,2048]{1,0:T(8,128)(2,1)S(1)}, u32[]{:S(2)}, u32[]{:S(2)}) %collective-permute-start.1) | collective-permute-done | bytes 524320 | tf_op jit(solution)/shard_map/ppermute | solution.py:315
  50.6 3.0 %collective-permute-start.7 = (bf16[512,896]{1,0:T(8,128)(2,1)S(1)}, bf16[512,896]{1,0:T(8,128)(2,1)S(1)}, u32[]{:S(2)}, u32[]{:S(2)}) collective-permute-start(bf16[512,896]{1,0:T(8,128)(2,1)S(1)} %constant_dynamic-update-slice_fusion.near_ref), channel_id=1, source_target_pairs={{0,16},{16,0},{32,48},{48,32},{64,80},{80,64},{96,112},{112,96},{1... | collective-permute-start | bytes 2752520 | tf_op jit(solution)/shard_map/ppermute | solution.py:312
  53.6 0.0 collective-permute-done.5.x3_ref
  53.6 3.3 %collective-permute-start.6 = (bf16[128,2048]{1,0:T(8,128)(2,1)S(1)}, bf16[128,2048]{1,0:T(8,128)(2,1)S(1)}, u32[]{:S(2)}, u32[]{:S(2)}) collective-permute-start(bf16[128,2048]{1,0:T(8,128)(2,1)S(1)} %collective-permute-done.5.x3_ref), channel_id=1, source_target_pairs={{0,12},{1,13},{2,14},{3,15},{4,0},{5,1},{6,2},{7,3},{8,4},{9,5},{1... | collective-permute-start | bytes 1572872 | tf_op jit(solution)/shard_map/ppermute | solution.py:315
  57.0 0.0 copy-start
  57.0 0.0 copy-start.1
  57.0 0.0 copy-start.2
  57.0 0.0 copy-start.3
  57.0 0.0 copy-start.4
  57.0 0.0 copy-start.5
  57.0 0.0 copy-start.6
  57.0 5.3 %collective-permute-start.4 = (bf16[128,896]{1,0:T(8,128)(2,1)S(1)}, bf16[128,896]{1,0:T(8,128)(2,1)S(1)}, u32[]{:S(2)}, u32[]{:S(2)}) collective-permute-start(bf16[128,896]{1,0:T(8,128)(2,1)S(1)} %slice.4), channel_id=1, source_target_pairs={{0,64},{32,96},{64,128},{96,160},{128,192},{160,224},{192,256},{22... | collective-permute-start | bytes 688136 | tf_op jit(solution)/shard_map/ppermute | solution.py:309
  62.4 5.4 %collective-permute-done.4.last_ref = bf16[128,896]{1,0:T(8,128)(2,1)S(1)} collective-permute-done((bf16[128,896]{1,0:T(8,128)(2,1)S(1)}, bf16[128,896]{1,0:T(8,128)(2,1)S(1)}, u32[]{:S(2)}, u32[]{:S(2)}) %collective-permute-start.4) | collective-permute-done | bytes 229408 | tf_op jit(solution)/shard_map/ppermute | solution.py:309
  67.7 1.3 %collective-permute-done.6.x2_ref = bf16[128,2048]{1,0:T(8,128)(2,1)S(1)} collective-permute-done((bf16[128,2048]{1,0:T(8,128)(2,1)S(1)}, bf16[128,2048]{1,0:T(8,128)(2,1)S(1)}, u32[]{:S(2)}, u32[]{:S(2)}) %collective-permute-start.6) | collective-permute-done | bytes 524320 | tf_op jit(solution)/shard_map/ppermute | solution.py:315
  69.1 0.0 collective-permute-done.3.far_ref
  69.1 0.0 collective-permute-done.7.other_near_ref
  69.1 3.6 %collective-permute-start.8 = (bf16[512,896]{1,0:T(8,128)(2,1)S(1)}, bf16[512,896]{1,0:T(8,128)(2,1)S(1)}, u32[]{:S(2)}, u32[]{:S(2)}) collective-permute-start(bf16[512,896]{1,0:T(8,128)(2,1)S(1)} %collective-permute-done.3.far_ref), channel_id=1, source_target_pairs={{0,16},{16,0},{32,48},{48,32},{64,80},{80,64},{96,112},{112,96},{1... | collective-permute-start | bytes 2752520 | tf_op jit(solution)/shard_map/ppermute | solution.py:312
  72.7 2.1 %shard_map.146 = (f32[512,896]{1,0:T(8,128)S(1)}, bf16[512,512]{1,0:T(8,128)(2,1)S(1)}) custom-call(bf16[128,2048]{1,0:T(8,128)(2,1)S(1)} %all_gather.7.x0_ref, bf16[128,2048]{1,0:T(8,128)(2,1)S(1)} %collective-permute-done.1.x1_ref, bf16[128,2048]{1,0:T(8,128)(2,1)S(1)} %collective-permute-done.6.x2_ref, ...), custom_call_target="tpu_custom_call" | custom-call | flops 1409286144 | bytes 8388608 | tf_op jit(solution)/shard_map/pallas_call | solution.py:334
  74.8 0.0 collective-permute-done.8.other_far_ref
  74.9 5.4 %shard_map.147 = bf16[512,256]{1,0:T(8,128)(2,1)S(1)} custom-call(f32[2]{0:T(128)S(1)} %copy-done.4, f32[2]{0:T(128)S(1)} %copy-done.5, f32[512,896]{1,0:T(8,128)S(1)} %get-tuple-element.29.sum_ref, bf16[512,512]{1,0:T(8,128)(2,1)S(1)} %get-tuple-element.30.left_ref, bf16[512,896]{1,0:T(8,128)(2,1)S(1)} %collective-permute-done.8.other_far_ref, ...), custom_call_target="tpu_custom_call" | custom-call | tf_op jit(solution)/shard_map/pallas_call | solution.py:346
  80.3 13.6 %all_to_all.19 = bf16[16,32,256]{2,1,0:T(8,128)(2,1)S(1)} all-to-all(bf16[16,32,256]{2,1,0:T(8,128)(2,1)S(1)} %bitcast.8), channel_id=1, replica_groups=mesh['dp'=32,'tp'=16] {'tp'}, dimensions={0} | all-to-all | bytes 524288 | tf_op jit(solution)/shard_map/all_to_all | solution.py:354
  93.8 0.7 copy.17
  (12 shorter events, 0.2 us)
Async XLA Ops:
  11.2 18.4 %collective-permute-start = (bf16[128,896]{1,0:T(8,128)(2,1)S(1)}, bf16[128,896]{1,0:T(8,128)(2,1)S(1)}, u32[]{:S(2)}, u32[]{:S(2)}) collective-permute-start(bf16[128,896]{1,0:T(8,128)(2,1)S(1)} %all_gather.6), channel_id=1, source_target_pairs={{0,128},{32,160},{64,192},{96,224},{128,256},{160,288},{192,320},{... | collective-permute-start | bytes 688136 | tf_op jit(solution)/shard_map/ppermute | solution.py:309
  29.6 15.4 %collective-permute-start.2 = (bf16[256,896]{1,0:T(8,128)(2,1)S(1)}, bf16[256,896]{1,0:T(8,128)(2,1)S(1)}, u32[]{:S(2)}, u32[]{:S(2)}) collective-permute-start(bf16[256,896]{1,0:T(8,128)(2,1)S(1)} %pad_maximum_fusion), channel_id=1, source_target_pairs={{0,64},{32,96},{64,128},{96,160},{128,192},{160,224},{192,256},{22... | collective-permute-start | bytes 1376264 | tf_op jit(solution)/shard_map/ppermute | solution.py:309
  34.3 16.4 %collective-permute-start.1 = (bf16[128,2048]{1,0:T(8,128)(2,1)S(1)}, bf16[128,2048]{1,0:T(8,128)(2,1)S(1)}, u32[]{:S(2)}, u32[]{:S(2)}) collective-permute-start(bf16[128,2048]{1,0:T(8,128)(2,1)S(1)} %all_gather.7.x0_ref), channel_id=1, source_target_pairs={{0,4},{1,5},{2,6},{3,7},{4,8},{5,9},{6,10},{7,11},{8,12},{9,13},{1... | collective-permute-start | bytes 1572872 | tf_op jit(solution)/shard_map/ppermute | solution.py:315
  37.3 16.3 %collective-permute-start.5 = (bf16[128,2048]{1,0:T(8,128)(2,1)S(1)}, bf16[128,2048]{1,0:T(8,128)(2,1)S(1)}, u32[]{:S(2)}, u32[]{:S(2)}) collective-permute-start(bf16[128,2048]{1,0:T(8,128)(2,1)S(1)} %all_gather.7.x0_ref), channel_id=1, source_target_pairs={{0,12},{1,13},{2,14},{3,15},{4,0},{5,1},{6,2},{7,3},{8,4},{9,5},{1... | collective-permute-start | bytes 1572872 | tf_op jit(solution)/shard_map/ppermute | solution.py:315
  45.0 24.0 %collective-permute-start.3 = (bf16[512,896]{1,0:T(8,128)(2,1)S(1)}, bf16[512,896]{1,0:T(8,128)(2,1)S(1)}, u32[]{:S(2)}, u32[]{:S(2)}) collective-permute-start(bf16[512,896]{1,0:T(8,128)(2,1)S(1)} %constant_dynamic-update-slice_fusion.near_ref), channel_id=1, source_target_pairs={{0,32},{32,64},{64,96},{96,128},{128,160},{160,192},{192,224},{224... | collective-permute-start | bytes 2752520 | tf_op jit(solution)/shard_map/ppermute | solution.py:309
  50.6 18.4 %collective-permute-start.7 = (bf16[512,896]{1,0:T(8,128)(2,1)S(1)}, bf16[512,896]{1,0:T(8,128)(2,1)S(1)}, u32[]{:S(2)}, u32[]{:S(2)}) collective-permute-start(bf16[512,896]{1,0:T(8,128)(2,1)S(1)} %constant_dynamic-update-slice_fusion.near_ref), channel_id=1, source_target_pairs={{0,16},{16,0},{32,48},{48,32},{64,80},{80,64},{96,112},{112,96},{1... | collective-permute-start | bytes 2752520 | tf_op jit(solution)/shard_map/ppermute | solution.py:312
  53.6 15.4 %collective-permute-start.6 = (bf16[128,2048]{1,0:T(8,128)(2,1)S(1)}, bf16[128,2048]{1,0:T(8,128)(2,1)S(1)}, u32[]{:S(2)}, u32[]{:S(2)}) collective-permute-start(bf16[128,2048]{1,0:T(8,128)(2,1)S(1)} %collective-permute-done.5.x3_ref), channel_id=1, source_target_pairs={{0,12},{1,13},{2,14},{3,15},{4,0},{5,1},{6,2},{7,3},{8,4},{9,5},{1... | collective-permute-start | bytes 1572872 | tf_op jit(solution)/shard_map/ppermute | solution.py:315
  57.0 17.8 %copy-start = (f32[4,256]{1,0:T(4,128)S(1)}, f32[4,256]{1,0:T(4,128)}, u32[]{:S(2)}) copy-start(f32[4,256]{1,0:T(4,128)} %tv_ref.1) | copy-start | bytes 12292
  57.0 17.8 %copy-start.1 = (s32[1,512]{1,0:T(1,128)S(1)}, s32[1,512]{1,0:T(1,128)}, u32[]{:S(2)}) copy-start(s32[1,512]{1,0:T(1,128)} %seg_ref.1) | copy-start | bytes 6148
  57.0 17.8 %copy-start.2 = (f32[4,128]{1,0:T(4,128)S(1)}, f32[4,128]{1,0:T(4,128)}, u32[]{:S(2)}) copy-start(f32[4,128]{1,0:T(4,128)} %tq_ref.1) | copy-start | bytes 6148
  57.0 17.8 %copy-start.3 = (f32[4,128]{1,0:T(4,128)S(1)}, f32[4,128]{1,0:T(4,128)}, u32[]{:S(2)}) copy-start(f32[4,128]{1,0:T(4,128)} %tk_ref.1) | copy-start | bytes 6148
  57.0 17.8 %copy-start.4 = (f32[2]{0:T(128)S(1)}, f32[2]{0:T(128)}, u32[]{:S(2)}) copy-start(f32[2]{0:T(128)} %rate_ref.1) | copy-start | bytes 28
  57.0 17.8 %copy-start.5 = (f32[2]{0:T(128)S(1)}, f32[2]{0:T(128)}, u32[]{:S(2)}) copy-start(f32[2]{0:T(128)} %bias_ref.1) | copy-start | bytes 28
  57.0 17.8 %copy-start.6 = (f32[128]{0:T(128)S(1)}, f32[128]{0:T(128)}, u32[]{:S(2)}) copy-start(f32[128]{0:T(128)} %param.28) | copy-start | bytes 1540
  57.0 10.7 %collective-permute-start.4 = (bf16[128,896]{1,0:T(8,128)(2,1)S(1)}, bf16[128,896]{1,0:T(8,128)(2,1)S(1)}, u32[]{:S(2)}, u32[]{:S(2)}) collective-permute-start(bf16[128,896]{1,0:T(8,128)(2,1)S(1)} %slice.4), channel_id=1, source_target_pairs={{0,64},{32,96},{64,128},{96,160},{128,192},{160,224},{192,256},{22... | collective-permute-start | bytes 688136 | tf_op jit(solution)/shard_map/ppermute | solution.py:309
  69.1 5.7 %collective-permute-start.8 = (bf16[512,896]{1,0:T(8,128)(2,1)S(1)}, bf16[512,896]{1,0:T(8,128)(2,1)S(1)}, u32[]{:S(2)}, u32[]{:S(2)}) collective-permute-start(bf16[512,896]{1,0:T(8,128)(2,1)S(1)} %collective-permute-done.3.far_ref), channel_id=1, source_target_pairs={{0,16},{16,0},{32,48},{48,32},{64,80},{80,64},{96,112},{112,96},{1... | collective-permute-start | bytes 2752520 | tf_op jit(solution)/shard_map/ppermute | solution.py:312

commit v4 on v3

--- a/solution.py
+++ b/solution.py
@@ -81,15 +81,17 @@
     copies = [pltpu.make_async_copy(source, target, sems.at[i]) for i, (source, target) in enumerate(moves)]
     for copy in copies:
         copy.start()
-    for copy in copies:
-        copy.wait()
     narrow = jnp.concatenate([beta_ref[...], decay_ref[...]], axis=0).astype(jnp.float32)
     narrow = jnp.concatenate([narrow, jnp.zeros((4, 64), jnp.float32)], axis=1)
     narrow = jnp.concatenate([narrow, jnp.zeros((124, 128), jnp.float32)], axis=0).T
-    joined_ref[:, 768:896] = narrow[:64].astype(jnp.bfloat16)
+    copies[0].wait()
+    copies[1].wait()
     floats = tokens_ref[...].astype(jnp.float32)
     scaled = floats * lax.rsqrt(jnp.mean(floats * floats, axis=-1, keepdims=True) + 1e-06)
     normed_ref[...] = (scaled * norm_ref[...]).astype(jnp.bfloat16)
+    for copy in copies[2:]:
+        copy.wait()
+    joined_ref[:, 768:896] = narrow[:64].astype(jnp.bfloat16)
 
 
 def project_kernel(

time: 95 us -> 95 us (level)
  no operation moved by 1% of the time
where the time goes in v4:
time: 95 us; the launch traced here: 94.6 us
  starting transfers between devices  37.9 us (40%)
  blocking collectives  33.6 us (35%)
  waiting for transfers between devices  11.9 us (13%)
  Pallas kernels  9.97 us (10%)
    ppermute x4, starting transfers between devices, along_z(): return lax.ppermute(block, 'dp', up + down)  21.5 us
    all_to_all x1, blocking collectives, shards(): return lax.all_to_all(tiles, 'tp', split_axis=0, concat_axis=1, tiled=True)  13.6 us
    all_gather x1, blocking collectives, shards(): lax.all_gather(normed, 'tp', axis=0, tiled=True, axis_index_groups=lines)  11.3 us
    ppermute x3, starting transfers between devices, along_x(): lax.ppermute(block, 'tp', [(i, (i + 4 * shift) % 16) for i in range(16)])  9.79 us
    ppermute x4, waiting for transfers between devices, along_z(): return lax.ppermute(block, 'dp', up + down)  9.5 us
    all_gather x1, blocking collectives, shards(): lax.all_gather(joined, 'dp', axis=0, tiled=True, axis_index_groups=chips)  8.7 us
    ppermute x2, starting transfers between devices, to_other_core(): return lax.ppermute(block, 'dp', [(i, i ^ 1) for i in range(32)])  6.58 us
    pallas_call x1, Pallas kernels, shards(): pl.pallas_call(mix_kernel, out_shape=jax.ShapeDtypeStruct((512, 256), jnp...  5.39 us
  transfers between devices with their start and end apart: 9, of which 4 were waited for; matrix products, arithmetic and copies ran while one was open for 0% of the time, Pallas kernels for 2%

profile of v4, /device:TPU:1, one launch (start us, length us, event | category | flops | bytes accessed | tf_op | source)
XLA Modules:
  0.0 94.6 jit_solution(11759110157126127877)
XLA Ops:
  0.0 2.5 %shard_map.145 = (bf16[64,896]{1,0:T(8,128)(2,1)}, bf16[32,2048]{1,0:T(8,128)(2,1)}) custom-call(bf16[32,2048]{1,0:T(8,128)(2,1)} %tokens_hbm.1, f32[1,2048]{1,0:T(1,128)} %bitcast.11, bf16[64,128]{1,0:T(8,128)(2,1)} %query_hbm.1, bf16[64,128]{1,0:T(8,128)(2,1)} %key_hbm.1, bf16[64,256]{1,0:T(8,128)(2,1)} %value_hbm.1, bf16[64,256]{1,0:T(8,128)(2,1)} %gate_hbm.1, ...), custom_call_target="tpu_custom_call" | custom-call | tf_op jit(solution)/shard_map/pallas_call | solution.py:292
  2.5 8.7 %all_gather.6 = bf16[128,896]{1,0:T(8,128)(2,1)S(1)} all-gather(bf16[64,896]{1,0:T(8,128)(2,1)} %get-tuple-element.18), channel_id=1, replica_groups={{0,16},{32,48},{64,80},{96,112},{128,144},{160,176},{192,208},{224,240}..., dimensions={0}, use_global_device_ids=true | all-gather | bytes 344064 | tf_op jit(solution)/shard_map/all_gather | solution.py:321
  11.2 7.1 %collective-permute-start = (bf16[128,896]{1,0:T(8,128)(2,1)S(1)}, bf16[128,896]{1,0:T(8,128)(2,1)S(1)}, u32[]{:S(2)}, u32[]{:S(2)}) collective-permute-start(bf16[128,896]{1,0:T(8,128)(2,1)S(1)} %all_gather.6), channel_id=1, source_target_pairs={{0,128},{32,160},{64,192},{96,224},{128,256},{160,288},{192,320},{... | collective-permute-start | bytes 688136 | tf_op jit(solution)/shard_map/ppermute | solution.py:311
  18.3 11.3 %all_gather.7.x0_ref = bf16[128,2048]{1,0:T(8,128)(2,1)S(1)} all-gather(bf16[32,2048]{1,0:T(8,128)(2,1)} %get-tuple-element.19), channel_id=1, replica_groups={{0,1,2,3},{4,5,6,7},{8,9,10,11},{12,13,14,15},{16,17,18,19},{20,21,22,2..., dimensions={0}, use_global_device_ids=true | all-gather | bytes 655360 | tf_op jit(solution)/shard_map/all_gather | solution.py:323
  29.6 0.0 collective-permute-done
  29.6 4.7 %collective-permute-start.2 = (bf16[256,896]{1,0:T(8,128)(2,1)S(1)}, bf16[256,896]{1,0:T(8,128)(2,1)S(1)}, u32[]{:S(2)}, u32[]{:S(2)}) collective-permute-start(bf16[256,896]{1,0:T(8,128)(2,1)S(1)} %pad_maximum_fusion), channel_id=1, source_target_pairs={{0,64},{32,96},{64,128},{96,160},{128,192},{160,224},{192,256},{22... | collective-permute-start | bytes 1376264 | tf_op jit(solution)/shard_map/ppermute | solution.py:311
  34.3 3.1 %collective-permute-start.1 = (bf16[128,2048]{1,0:T(8,128)(2,1)S(1)}, bf16[128,2048]{1,0:T(8,128)(2,1)S(1)}, u32[]{:S(2)}, u32[]{:S(2)}) collective-permute-start(bf16[128,2048]{1,0:T(8,128)(2,1)S(1)} %all_gather.7.x0_ref), channel_id=1, source_target_pairs={{0,4},{1,5},{2,6},{3,7},{4,8},{5,9},{6,10},{7,11},{8,12},{9,13},{1... | collective-permute-start | bytes 1572872 | tf_op jit(solution)/shard_map/ppermute | solution.py:317
  37.3 3.4 %collective-permute-start.5 = (bf16[128,2048]{1,0:T(8,128)(2,1)S(1)}, bf16[128,2048]{1,0:T(8,128)(2,1)S(1)}, u32[]{:S(2)}, u32[]{:S(2)}) collective-permute-start(bf16[128,2048]{1,0:T(8,128)(2,1)S(1)} %all_gather.7.x0_ref), channel_id=1, source_target_pairs={{0,12},{1,13},{2,14},{3,15},{4,0},{5,1},{6,2},{7,3},{8,4},{9,5},{1... | collective-permute-start | bytes 1572872 | tf_op jit(solution)/shard_map/ppermute | solution.py:317
  40.8 4.1 %collective-permute-done.2 = bf16[256,896]{1,0:T(8,128)(2,1)S(1)} collective-permute-done((bf16[256,896]{1,0:T(8,128)(2,1)S(1)}, bf16[256,896]{1,0:T(8,128)(2,1)S(1)}, u32[]{:S(2)}, u32[]{:S(2)}) %collective-permute-start.2) | collective-permute-done | bytes 458784 | tf_op jit(solution)/shard_map/ppermute | solution.py:311
  45.0 4.5 %collective-permute-start.3 = (bf16[512,896]{1,0:T(8,128)(2,1)S(1)}, bf16[512,896]{1,0:T(8,128)(2,1)S(1)}, u32[]{:S(2)}, u32[]{:S(2)}) collective-permute-start(bf16[512,896]{1,0:T(8,128)(2,1)S(1)} %constant_dynamic-update-slice_fusion.near_ref), channel_id=1, source_target_pairs={{0,32},{32,64},{64,96},{96,128},{128,160},{160,192},{192,224},{224... | collective-permute-start | bytes 2752520 | tf_op jit(solution)/shard_map/ppermute | solution.py:311
  49.5 1.1 %collective-permute-done.1.x1_ref = bf16[128,2048]{1,0:T(8,128)(2,1)S(1)} collective-permute-done((bf16[128,2048]{1,0:T(8,128)(2,1)S(1)}, bf16[128,2048]{1,0:T(8,128)(2,1)S(1)}, u32[]{:S(2)}, u32[]{:S(2)}) %collective-permute-start.1) | collective-permute-done | bytes 524320 | tf_op jit(solution)/shard_map/ppermute | solution.py:317
  50.6 3.0 %collective-permute-start.7 = (bf16[512,896]{1,0:T(8,128)(2,1)S(1)}, bf16[512,896]{1,0:T(8,128)(2,1)S(1)}, u32[]{:S(2)}, u32[]{:S(2)}) collective-permute-start(bf16[512,896]{1,0:T(8,128)(2,1)S(1)} %constant_dynamic-update-slice_fusion.near_ref), channel_id=1, source_target_pairs={{0,16},{16,0},{32,48},{48,32},{64,80},{80,64},{96,112},{112,96},{1... | collective-permute-start | bytes 2752520 | tf_op jit(solution)/shard_map/ppermute | solution.py:314
  53.6 0.0 collective-permute-done.5.x3_ref
  53.6 3.3 %collective-permute-start.6 = (bf16[128,2048]{1,0:T(8,128)(2,1)S(1)}, bf16[128,2048]{1,0:T(8,128)(2,1)S(1)}, u32[]{:S(2)}, u32[]{:S(2)}) collective-permute-start(bf16[128,2048]{1,0:T(8,128)(2,1)S(1)} %collective-permute-done.5.x3_ref), channel_id=1, source_target_pairs={{0,12},{1,13},{2,14},{3,15},{4,0},{5,1},{6,2},{7,3},{8,4},{9,5},{1... | collective-permute-start | bytes 1572872 | tf_op jit(solution)/shard_map/ppermute | solution.py:317
  57.0 0.0 copy-start
  57.0 0.0 copy-start.1
  57.0 0.0 copy-start.2
  57.0 0.0 copy-start.3
  57.0 0.0 copy-start.4
  57.0 0.0 copy-start.5
  57.0 0.0 copy-start.6
  57.0 5.3 %collective-permute-start.4 = (bf16[128,896]{1,0:T(8,128)(2,1)S(1)}, bf16[128,896]{1,0:T(8,128)(2,1)S(1)}, u32[]{:S(2)}, u32[]{:S(2)}) collective-permute-start(bf16[128,896]{1,0:T(8,128)(2,1)S(1)} %slice.4), channel_id=1, source_target_pairs={{0,64},{32,96},{64,128},{96,160},{128,192},{160,224},{192,256},{22... | collective-permute-start | bytes 688136 | tf_op jit(solution)/shard_map/ppermute | solution.py:311
  62.4 5.4 %collective-permute-done.4.last_ref = bf16[128,896]{1,0:T(8,128)(2,1)S(1)} collective-permute-done((bf16[128,896]{1,0:T(8,128)(2,1)S(1)}, bf16[128,896]{1,0:T(8,128)(2,1)S(1)}, u32[]{:S(2)}, u32[]{:S(2)}) %collective-permute-start.4) | collective-permute-done | bytes 229408 | tf_op jit(solution)/shard_map/ppermute | solution.py:311
  67.7 1.3 %collective-permute-done.6.x2_ref = bf16[128,2048]{1,0:T(8,128)(2,1)S(1)} collective-permute-done((bf16[128,2048]{1,0:T(8,128)(2,1)S(1)}, bf16[128,2048]{1,0:T(8,128)(2,1)S(1)}, u32[]{:S(2)}, u32[]{:S(2)}) %collective-permute-start.6) | collective-permute-done | bytes 524320 | tf_op jit(solution)/shard_map/ppermute | solution.py:317
  69.1 0.0 collective-permute-done.3.far_ref
  69.1 0.0 collective-permute-done.7.other_near_ref
  69.1 3.6 %collective-permute-start.8 = (bf16[512,896]{1,0:T(8,128)(2,1)S(1)}, bf16[512,896]{1,0:T(8,128)(2,1)S(1)}, u32[]{:S(2)}, u32[]{:S(2)}) collective-permute-start(bf16[512,896]{1,0:T(8,128)(2,1)S(1)} %collective-permute-done.3.far_ref), channel_id=1, source_target_pairs={{0,16},{16,0},{32,48},{48,32},{64,80},{80,64},{96,112},{112,96},{1... | collective-permute-start | bytes 2752520 | tf_op jit(solution)/shard_map/ppermute | solution.py:314
  72.7 2.1 %shard_map.146 = (f32[512,896]{1,0:T(8,128)S(1)}, bf16[512,512]{1,0:T(8,128)(2,1)S(1)}) custom-call(bf16[128,2048]{1,0:T(8,128)(2,1)S(1)} %all_gather.7.x0_ref, bf16[128,2048]{1,0:T(8,128)(2,1)S(1)} %collective-permute-done.1.x1_ref, bf16[128,2048]{1,0:T(8,128)(2,1)S(1)} %collective-permute-done.6.x2_ref, ...), custom_call_target="tpu_custom_call" | custom-call | flops 1409286144 | bytes 8388608 | tf_op jit(solution)/shard_map/pallas_call | solution.py:336
  74.8 0.0 collective-permute-done.8.other_far_ref
  74.9 5.4 %shard_map.147 = bf16[512,256]{1,0:T(8,128)(2,1)S(1)} custom-call(f32[2]{0:T(128)S(1)} %copy-done.4, f32[2]{0:T(128)S(1)} %copy-done.5, f32[512,896]{1,0:T(8,128)S(1)} %get-tuple-element.29.sum_ref, bf16[512,512]{1,0:T(8,128)(2,1)S(1)} %get-tuple-element.30.left_ref, bf16[512,896]{1,0:T(8,128)(2,1)S(1)} %collective-permute-done.8.other_far_ref, ...), custom_call_target="tpu_custom_call" | custom-call | tf_op jit(solution)/shard_map/pallas_call | solution.py:348
  80.3 13.6 %all_to_all.19 = bf16[16,32,256]{2,1,0:T(8,128)(2,1)S(1)} all-to-all(bf16[16,32,256]{2,1,0:T(8,128)(2,1)S(1)} %bitcast.8), channel_id=1, replica_groups=mesh['dp'=32,'tp'=16] {'tp'}, dimensions={0} | all-to-all | bytes 524288 | tf_op jit(solution)/shard_map/all_to_all | solution.py:356
  93.9 0.7 copy.17
  (12 shorter events, 0.2 us)
Async XLA Ops:
  11.2 18.4 %collective-permute-start = (bf16[128,896]{1,0:T(8,128)(2,1)S(1)}, bf16[128,896]{1,0:T(8,128)(2,1)S(1)}, u32[]{:S(2)}, u32[]{:S(2)}) collective-permute-start(bf16[128,896]{1,0:T(8,128)(2,1)S(1)} %all_gather.6), channel_id=1, source_target_pairs={{0,128},{32,160},{64,192},{96,224},{128,256},{160,288},{192,320},{... | collective-permute-start | bytes 688136 | tf_op jit(solution)/shard_map/ppermute | solution.py:311
  29.6 15.4 %collective-permute-start.2 = (bf16[256,896]{1,0:T(8,128)(2,1)S(1)}, bf16[256,896]{1,0:T(8,128)(2,1)S(1)}, u32[]{:S(2)}, u32[]{:S(2)}) collective-permute-start(bf16[256,896]{1,0:T(8,128)(2,1)S(1)} %pad_maximum_fusion), channel_id=1, source_target_pairs={{0,64},{32,96},{64,128},{96,160},{128,192},{160,224},{192,256},{22... | collective-permute-start | bytes 1376264 | tf_op jit(solution)/shard_map/ppermute | solution.py:311
  34.3 16.4 %collective-permute-start.1 = (bf16[128,2048]{1,0:T(8,128)(2,1)S(1)}, bf16[128,2048]{1,0:T(8,128)(2,1)S(1)}, u32[]{:S(2)}, u32[]{:S(2)}) collective-permute-start(bf16[128,2048]{1,0:T(8,128)(2,1)S(1)} %all_gather.7.x0_ref), channel_id=1, source_target_pairs={{0,4},{1,5},{2,6},{3,7},{4,8},{5,9},{6,10},{7,11},{8,12},{9,13},{1... | collective-permute-start | bytes 1572872 | tf_op jit(solution)/shard_map/ppermute | solution.py:317
  37.3 16.3 %collective-permute-start.5 = (bf16[128,2048]{1,0:T(8,128)(2,1)S(1)}, bf16[128,2048]{1,0:T(8,128)(2,1)S(1)}, u32[]{:S(2)}, u32[]{:S(2)}) collective-permute-start(bf16[128,2048]{1,0:T(8,128)(2,1)S(1)} %all_gather.7.x0_ref), channel_id=1, source_target_pairs={{0,12},{1,13},{2,14},{3,15},{4,0},{5,1},{6,2},{7,3},{8,4},{9,5},{1... | collective-permute-start | bytes 1572872 | tf_op jit(solution)/shard_map/ppermute | solution.py:317
  45.0 24.0 %collective-permute-start.3 = (bf16[512,896]{1,0:T(8,128)(2,1)S(1)}, bf16[512,896]{1,0:T(8,128)(2,1)S(1)}, u32[]{:S(2)}, u32[]{:S(2)}) collective-permute-start(bf16[512,896]{1,0:T(8,128)(2,1)S(1)} %constant_dynamic-update-slice_fusion.near_ref), channel_id=1, source_target_pairs={{0,32},{32,64},{64,96},{96,128},{128,160},{160,192},{192,224},{224... | collective-permute-start | bytes 2752520 | tf_op jit(solution)/shard_map/ppermute | solution.py:311
  50.6 18.4 %collective-permute-start.7 = (bf16[512,896]{1,0:T(8,128)(2,1)S(1)}, bf16[512,896]{1,0:T(8,128)(2,1)S(1)}, u32[]{:S(2)}, u32[]{:S(2)}) collective-permute-start(bf16[512,896]{1,0:T(8,128)(2,1)S(1)} %constant_dynamic-update-slice_fusion.near_ref), channel_id=1, source_target_pairs={{0,16},{16,0},{32,48},{48,32},{64,80},{80,64},{96,112},{112,96},{1... | collective-permute-start | bytes 2752520 | tf_op jit(solution)/shard_map/ppermute | solution.py:314
  53.6 15.4 %collective-permute-start.6 = (bf16[128,2048]{1,0:T(8,128)(2,1)S(1)}, bf16[128,2048]{1,0:T(8,128)(2,1)S(1)}, u32[]{:S(2)}, u32[]{:S(2)}) collective-permute-start(bf16[128,2048]{1,0:T(8,128)(2,1)S(1)} %collective-permute-done.5.x3_ref), channel_id=1, source_target_pairs={{0,12},{1,13},{2,14},{3,15},{4,0},{5,1},{6,2},{7,3},{8,4},{9,5},{1... | collective-permute-start | bytes 1572872 | tf_op jit(solution)/shard_map/ppermute | solution.py:317
  57.0 17.8 %copy-start = (f32[4,256]{1,0:T(4,128)S(1)}, f32[4,256]{1,0:T(4,128)}, u32[]{:S(2)}) copy-start(f32[4,256]{1,0:T(4,128)} %tv_ref.1) | copy-start | bytes 12292
  57.0 17.8 %copy-start.1 = (s32[1,512]{1,0:T(1,128)S(1)}, s32[1,512]{1,0:T(1,128)}, u32[]{:S(2)}) copy-start(s32[1,512]{1,0:T(1,128)} %seg_ref.1) | copy-start | bytes 6148
  57.0 17.8 %copy-start.2 = (f32[4,128]{1,0:T(4,128)S(1)}, f32[4,128]{1,0:T(4,128)}, u32[]{:S(2)}) copy-start(f32[4,128]{1,0:T(4,128)} %tq_ref.1) | copy-start | bytes 6148
  57.0 17.8 %copy-start.3 = (f32[4,128]{1,0:T(4,128)S(1)}, f32[4,128]{1,0:T(4,128)}, u32[]{:S(2)}) copy-start(f32[4,128]{1,0:T(4,128)} %tk_ref.1) | copy-start | bytes 6148
  57.0 17.8 %copy-start.4 = (f32[2]{0:T(128)S(1)}, f32[2]{0:T(128)}, u32[]{:S(2)}) copy-start(f32[2]{0:T(128)} %rate_ref.1) | copy-start | bytes 28
  57.0 17.8 %copy-start.5 = (f32[2]{0:T(128)S(1)}, f32[2]{0:T(128)}, u32[]{:S(2)}) copy-start(f32[2]{0:T(128)} %bias_ref.1) | copy-start | bytes 28
  57.0 17.8 %copy-start.6 = (f32[128]{0:T(128)S(1)}, f32[128]{0:T(128)}, u32[]{:S(2)}) copy-start(f32[128]{0:T(128)} %param.28) | copy-start | bytes 1540
  57.0 10.7 %collective-permute-start.4 = (bf16[128,896]{1,0:T(8,128)(2,1)S(1)}, bf16[128,896]{1,0:T(8,128)(2,1)S(1)}, u32[]{:S(2)}, u32[]{:S(2)}) collective-permute-start(bf16[128,896]{1,0:T(8,128)(2,1)S(1)} %slice.4), channel_id=1, source_target_pairs={{0,64},{32,96},{64,128},{96,160},{128,192},{160,224},{192,256},{22... | collective-permute-start | bytes 688136 | tf_op jit(solution)/shard_map/ppermute | solution.py:311
  69.1 5.7 %collective-permute-start.8 = (bf16[512,896]{1,0:T(8,128)(2,1)S(1)}, bf16[512,896]{1,0:T(8,128)(2,1)S(1)}, u32[]{:S(2)}, u32[]{:S(2)}) collective-permute-start(bf16[512,896]{1,0:T(8,128)(2,1)S(1)} %collective-permute-done.3.far_ref), channel_id=1, source_target_pairs={{0,16},{16,0},{32,48},{48,32},{64,80},{80,64},{96,112},{112,96},{1... | collective-permute-start | bytes 2752520 | tf_op jit(solution)/shard_map/ppermute | solution.py:314

commit v5 on v3

--- a/solution.py
+++ b/solution.py
@@ -67,22 +67,12 @@
 
 
 def pack_kernel(
-    tokens_hbm, norm_hbm, query_hbm, key_hbm, value_hbm, gate_hbm, beta_ref, decay_ref, joined_ref, normed_ref,
-    tokens_ref, norm_ref, sems
+    tokens_ref, norm_ref, query_ref, key_ref, value_ref, gate_ref, beta_ref, decay_ref, joined_ref, normed_ref
 ):
-    moves = (
-        (tokens_hbm, tokens_ref),
-        (norm_hbm, norm_ref),
-        (query_hbm, joined_ref.at[:, 0:128]),
-        (key_hbm, joined_ref.at[:, 128:256]),
-        (value_hbm, joined_ref.at[:, 256:512]),
-        (gate_hbm, joined_ref.at[:, 512:768]),
-    )
-    copies = [pltpu.make_async_copy(source, target, sems.at[i]) for i, (source, target) in enumerate(moves)]
-    for copy in copies:
-        copy.start()
-    for copy in copies:
-        copy.wait()
+    joined_ref[:, 0:128] = query_ref[...]
+    joined_ref[:, 128:256] = key_ref[...]
+    joined_ref[:, 256:512] = value_ref[...]
+    joined_ref[:, 512:768] = gate_ref[...]
     narrow = jnp.concatenate([beta_ref[...], decay_ref[...]], axis=0).astype(jnp.float32)
     narrow = jnp.concatenate([narrow, jnp.zeros((4, 64), jnp.float32)], axis=1)
     narrow = jnp.concatenate([narrow, jnp.zeros((124, 128), jnp.float32)], axis=0).T
@@ -293,13 +283,8 @@
             jax.ShapeDtypeStruct((64, 896), jnp.bfloat16),
             jax.ShapeDtypeStruct(tokens.shape, jnp.bfloat16),
         ),
-        in_specs=[pl.BlockSpec(memory_space=pl.ANY)] * 6 + [vmem] * 2,
+        in_specs=[vmem] * 8,
         out_specs=(vmem, vmem),
-        scratch_shapes=[
-            pltpu.VMEM(tokens.shape, jnp.bfloat16),
-            pltpu.VMEM((1, tokens.shape[1]), jnp.float32),
-            pltpu.SemaphoreType.DMA((6,)),
-        ],
         compiler_params=pltpu.CompilerParams(vmem_limit_bytes=58 * 1024 * 1024),
     )(tokens, norm_gain.reshape(1, -1), w_query, w_key, w_value, w_gate, w_beta.T, w_decay.T)
 

time: 95 us -> 94.3 us (level)
  no operation moved by 1% of the time
where the time goes in v5:
time: 94.3 us; the launch traced here: 93.9 us
  starting transfers between devices  37.9 us (40%)
  blocking collectives  33.6 us (36%)
  waiting for transfers between devices  11.9 us (13%)
  Pallas kernels  9.28 us (10%)
    ppermute x4, starting transfers between devices, along_z(): return lax.ppermute(block, 'dp', up + down)  21.5 us
    all_to_all x1, blocking collectives, shards(): return lax.all_to_all(tiles, 'tp', split_axis=0, concat_axis=1, tiled=True)  13.6 us
    all_gather x1, blocking collectives, shards(): lax.all_gather(normed, 'tp', axis=0, tiled=True, axis_index_groups=lines)  11.3 us
    ppermute x3, starting transfers between devices, along_x(): lax.ppermute(block, 'tp', [(i, (i + 4 * shift) % 16) for i in range(16)])  9.79 us
    ppermute x4, waiting for transfers between devices, along_z(): return lax.ppermute(block, 'dp', up + down)  9.5 us
    all_gather x1, blocking collectives, shards(): lax.all_gather(joined, 'dp', axis=0, tiled=True, axis_index_groups=chips)  8.69 us
    ppermute x2, starting transfers between devices, to_other_core(): return lax.ppermute(block, 'dp', [(i, i ^ 1) for i in range(32)])  6.58 us
    pallas_call x1, Pallas kernels, shards(): pl.pallas_call(mix_kernel, out_shape=jax.ShapeDtypeStruct((512, 256), jnp...  5.39 us
  transfers between devices with their start and end apart: 9, of which 4 were waited for; matrix products, arithmetic and copies ran while one was open for 0% of the time, Pallas kernels for 2%

profile of v5, /device:TPU:1, one launch (start us, length us, event | category | flops | bytes accessed | tf_op | source)
XLA Modules:
  0.0 93.9 jit_solution(1837046486061650005)
XLA Ops:
  0.0 1.8 %shard_map.145 = (bf16[64,896]{1,0:T(8,128)(2,1)}, bf16[32,2048]{1,0:T(8,128)(2,1)}) custom-call(bf16[32,2048]{1,0:T(8,128)(2,1)} %tokens_ref.1, f32[1,2048]{1,0:T(1,128)} %bitcast.11, bf16[64,128]{1,0:T(8,128)(2,1)} %query_ref.1, bf16[64,128]{1,0:T(8,128)(2,1)} %key_ref.1, bf16[64,256]{1,0:T(8,128)(2,1)} %value_ref.1, bf16[64,256]{1,0:T(8,128)(2,1)} %gate_ref.1, ...), custom_call_target="tpu_custom_call" | custom-call | tf_op jit(solution)/shard_map/pallas_call | solution.py:280
  1.8 8.7 %all_gather.6 = bf16[128,896]{1,0:T(8,128)(2,1)S(1)} all-gather(bf16[64,896]{1,0:T(8,128)(2,1)} %get-tuple-element.18), channel_id=1, replica_groups={{0,16},{32,48},{64,80},{96,112},{128,144},{160,176},{192,208},{224,240}..., dimensions={0}, use_global_device_ids=true | all-gather | bytes 344064 | tf_op jit(solution)/shard_map/all_gather | solution.py:304
  10.5 7.1 %collective-permute-start = (bf16[128,896]{1,0:T(8,128)(2,1)S(1)}, bf16[128,896]{1,0:T(8,128)(2,1)S(1)}, u32[]{:S(2)}, u32[]{:S(2)}) collective-permute-start(bf16[128,896]{1,0:T(8,128)(2,1)S(1)} %all_gather.6), channel_id=1, source_target_pairs={{0,128},{32,160},{64,192},{96,224},{128,256},{160,288},{192,320},{... | collective-permute-start | bytes 688136 | tf_op jit(solution)/shard_map/ppermute | solution.py:294
  17.6 11.3 %all_gather.7.x0_ref = bf16[128,2048]{1,0:T(8,128)(2,1)S(1)} all-gather(bf16[32,2048]{1,0:T(8,128)(2,1)} %get-tuple-element.19), channel_id=1, replica_groups={{0,1,2,3},{4,5,6,7},{8,9,10,11},{12,13,14,15},{16,17,18,19},{20,21,22,2..., dimensions={0}, use_global_device_ids=true | all-gather | bytes 655360 | tf_op jit(solution)/shard_map/all_gather | solution.py:306
  28.9 0.0 collective-permute-done
  28.9 4.7 %collective-permute-start.2 = (bf16[256,896]{1,0:T(8,128)(2,1)S(1)}, bf16[256,896]{1,0:T(8,128)(2,1)S(1)}, u32[]{:S(2)}, u32[]{:S(2)}) collective-permute-start(bf16[256,896]{1,0:T(8,128)(2,1)S(1)} %pad_maximum_fusion), channel_id=1, source_target_pairs={{0,64},{32,96},{64,128},{96,160},{128,192},{160,224},{192,256},{22... | collective-permute-start | bytes 1376264 | tf_op jit(solution)/shard_map/ppermute | solution.py:294
  33.6 3.1 %collective-permute-start.1 = (bf16[128,2048]{1,0:T(8,128)(2,1)S(1)}, bf16[128,2048]{1,0:T(8,128)(2,1)S(1)}, u32[]{:S(2)}, u32[]{:S(2)}) collective-permute-start(bf16[128,2048]{1,0:T(8,128)(2,1)S(1)} %all_gather.7.x0_ref), channel_id=1, source_target_pairs={{0,4},{1,5},{2,6},{3,7},{4,8},{5,9},{6,10},{7,11},{8,12},{9,13},{1... | collective-permute-start | bytes 1572872 | tf_op jit(solution)/shard_map/ppermute | solution.py:300
  36.6 3.4 %collective-permute-start.5 = (bf16[128,2048]{1,0:T(8,128)(2,1)S(1)}, bf16[128,2048]{1,0:T(8,128)(2,1)S(1)}, u32[]{:S(2)}, u32[]{:S(2)}) collective-permute-start(bf16[128,2048]{1,0:T(8,128)(2,1)S(1)} %all_gather.7.x0_ref), channel_id=1, source_target_pairs={{0,12},{1,13},{2,14},{3,15},{4,0},{5,1},{6,2},{7,3},{8,4},{9,5},{1... | collective-permute-start | bytes 1572872 | tf_op jit(solution)/shard_map/ppermute | solution.py:300
  40.1 4.1 %collective-permute-done.2 = bf16[256,896]{1,0:T(8,128)(2,1)S(1)} collective-permute-done((bf16[256,896]{1,0:T(8,128)(2,1)S(1)}, bf16[256,896]{1,0:T(8,128)(2,1)S(1)}, u32[]{:S(2)}, u32[]{:S(2)}) %collective-permute-start.2) | collective-permute-done | bytes 458784 | tf_op jit(solution)/shard_map/ppermute | solution.py:294
  44.3 4.5 %collective-permute-start.3 = (bf16[512,896]{1,0:T(8,128)(2,1)S(1)}, bf16[512,896]{1,0:T(8,128)(2,1)S(1)}, u32[]{:S(2)}, u32[]{:S(2)}) collective-permute-start(bf16[512,896]{1,0:T(8,128)(2,1)S(1)} %constant_dynamic-update-slice_fusion.near_ref), channel_id=1, source_target_pairs={{0,32},{32,64},{64,96},{96,128},{128,160},{160,192},{192,224},{224... | collective-permute-start | bytes 2752520 | tf_op jit(solution)/shard_map/ppermute | solution.py:294
  48.8 1.1 %collective-permute-done.1.x1_ref = bf16[128,2048]{1,0:T(8,128)(2,1)S(1)} collective-permute-done((bf16[128,2048]{1,0:T(8,128)(2,1)S(1)}, bf16[128,2048]{1,0:T(8,128)(2,1)S(1)}, u32[]{:S(2)}, u32[]{:S(2)}) %collective-permute-start.1) | collective-permute-done | bytes 524320 | tf_op jit(solution)/shard_map/ppermute | solution.py:300
  49.9 3.0 %collective-permute-start.7 = (bf16[512,896]{1,0:T(8,128)(2,1)S(1)}, bf16[512,896]{1,0:T(8,128)(2,1)S(1)}, u32[]{:S(2)}, u32[]{:S(2)}) collective-permute-start(bf16[512,896]{1,0:T(8,128)(2,1)S(1)} %constant_dynamic-update-slice_fusion.near_ref), channel_id=1, source_target_pairs={{0,16},{16,0},{32,48},{48,32},{64,80},{80,64},{96,112},{112,96},{1... | collective-permute-start | bytes 2752520 | tf_op jit(solution)/shard_map/ppermute | solution.py:297
  52.9 0.0 collective-permute-done.5.x3_ref
  52.9 3.3 %collective-permute-start.6 = (bf16[128,2048]{1,0:T(8,128)(2,1)S(1)}, bf16[128,2048]{1,0:T(8,128)(2,1)S(1)}, u32[]{:S(2)}, u32[]{:S(2)}) collective-permute-start(bf16[128,2048]{1,0:T(8,128)(2,1)S(1)} %collective-permute-done.5.x3_ref), channel_id=1, source_target_pairs={{0,12},{1,13},{2,14},{3,15},{4,0},{5,1},{6,2},{7,3},{8,4},{9,5},{1... | collective-permute-start | bytes 1572872 | tf_op jit(solution)/shard_map/ppermute | solution.py:300
  56.3 0.0 copy-start
  56.3 0.0 copy-start.1
  56.3 0.0 copy-start.2
  56.3 0.0 copy-start.3
  56.3 0.0 copy-start.4
  56.3 0.0 copy-start.5
  56.3 0.0 copy-start.6
  56.4 5.3 %collective-permute-start.4 = (bf16[128,896]{1,0:T(8,128)(2,1)S(1)}, bf16[128,896]{1,0:T(8,128)(2,1)S(1)}, u32[]{:S(2)}, u32[]{:S(2)}) collective-permute-start(bf16[128,896]{1,0:T(8,128)(2,1)S(1)} %slice.4), channel_id=1, source_target_pairs={{0,64},{32,96},{64,128},{96,160},{128,192},{160,224},{192,256},{22... | collective-permute-start | bytes 688136 | tf_op jit(solution)/shard_map/ppermute | solution.py:294
  61.7 5.4 %collective-permute-done.4.last_ref = bf16[128,896]{1,0:T(8,128)(2,1)S(1)} collective-permute-done((bf16[128,896]{1,0:T(8,128)(2,1)S(1)}, bf16[128,896]{1,0:T(8,128)(2,1)S(1)}, u32[]{:S(2)}, u32[]{:S(2)}) %collective-permute-start.4) | collective-permute-done | bytes 229408 | tf_op jit(solution)/shard_map/ppermute | solution.py:294
  67.0 1.3 %collective-permute-done.6.x2_ref = bf16[128,2048]{1,0:T(8,128)(2,1)S(1)} collective-permute-done((bf16[128,2048]{1,0:T(8,128)(2,1)S(1)}, bf16[128,2048]{1,0:T(8,128)(2,1)S(1)}, u32[]{:S(2)}, u32[]{:S(2)}) %collective-permute-start.6) | collective-permute-done | bytes 524320 | tf_op jit(solution)/shard_map/ppermute | solution.py:300
  68.4 0.0 collective-permute-done.3.far_ref
  68.4 0.0 collective-permute-done.7.other_near_ref
  68.4 3.6 %collective-permute-start.8 = (bf16[512,896]{1,0:T(8,128)(2,1)S(1)}, bf16[512,896]{1,0:T(8,128)(2,1)S(1)}, u32[]{:S(2)}, u32[]{:S(2)}) collective-permute-start(bf16[512,896]{1,0:T(8,128)(2,1)S(1)} %collective-permute-done.3.far_ref), channel_id=1, source_target_pairs={{0,16},{16,0},{32,48},{48,32},{64,80},{80,64},{96,112},{112,96},{1... | collective-permute-start | bytes 2752520 | tf_op jit(solution)/shard_map/ppermute | solution.py:297
  72.0 2.1 %shard_map.146 = (f32[512,896]{1,0:T(8,128)S(1)}, bf16[512,512]{1,0:T(8,128)(2,1)S(1)}) custom-call(bf16[128,2048]{1,0:T(8,128)(2,1)S(1)} %all_gather.7.x0_ref, bf16[128,2048]{1,0:T(8,128)(2,1)S(1)} %collective-permute-done.1.x1_ref, bf16[128,2048]{1,0:T(8,128)(2,1)S(1)} %collective-permute-done.6.x2_ref, ...), custom_call_target="tpu_custom_call" | custom-call | flops 1409286144 | bytes 8388608 | tf_op jit(solution)/shard_map/pallas_call | solution.py:319
  74.1 0.0 collective-permute-done.8.other_far_ref
  74.2 5.4 %shard_map.147 = bf16[512,256]{1,0:T(8,128)(2,1)S(1)} custom-call(f32[2]{0:T(128)S(1)} %copy-done.4, f32[2]{0:T(128)S(1)} %copy-done.5, f32[512,896]{1,0:T(8,128)S(1)} %get-tuple-element.29.sum_ref, bf16[512,512]{1,0:T(8,128)(2,1)S(1)} %get-tuple-element.30.left_ref, bf16[512,896]{1,0:T(8,128)(2,1)S(1)} %collective-permute-done.8.other_far_ref, ...), custom_call_target="tpu_custom_call" | custom-call | tf_op jit(solution)/shard_map/pallas_call | solution.py:331
  79.6 13.6 %all_to_all.19 = bf16[16,32,256]{2,1,0:T(8,128)(2,1)S(1)} all-to-all(bf16[16,32,256]{2,1,0:T(8,128)(2,1)S(1)} %bitcast.8), channel_id=1, replica_groups=mesh['dp'=32,'tp'=16] {'tp'}, dimensions={0} | all-to-all | bytes 524288 | tf_op jit(solution)/shard_map/all_to_all | solution.py:339
  93.1 0.7 copy.17
  (12 shorter events, 0.2 us)
Async XLA Ops:
  10.5 18.4 %collective-permute-start = (bf16[128,896]{1,0:T(8,128)(2,1)S(1)}, bf16[128,896]{1,0:T(8,128)(2,1)S(1)}, u32[]{:S(2)}, u32[]{:S(2)}) collective-permute-start(bf16[128,896]{1,0:T(8,128)(2,1)S(1)} %all_gather.6), channel_id=1, source_target_pairs={{0,128},{32,160},{64,192},{96,224},{128,256},{160,288},{192,320},{... | collective-permute-start | bytes 688136 | tf_op jit(solution)/shard_map/ppermute | solution.py:294
  28.9 15.4 %collective-permute-start.2 = (bf16[256,896]{1,0:T(8,128)(2,1)S(1)}, bf16[256,896]{1,0:T(8,128)(2,1)S(1)}, u32[]{:S(2)}, u32[]{:S(2)}) collective-permute-start(bf16[256,896]{1,0:T(8,128)(2,1)S(1)} %pad_maximum_fusion), channel_id=1, source_target_pairs={{0,64},{32,96},{64,128},{96,160},{128,192},{160,224},{192,256},{22... | collective-permute-start | bytes 1376264 | tf_op jit(solution)/shard_map/ppermute | solution.py:294
  33.6 16.4 %collective-permute-start.1 = (bf16[128,2048]{1,0:T(8,128)(2,1)S(1)}, bf16[128,2048]{1,0:T(8,128)(2,1)S(1)}, u32[]{:S(2)}, u32[]{:S(2)}) collective-permute-start(bf16[128,2048]{1,0:T(8,128)(2,1)S(1)} %all_gather.7.x0_ref), channel_id=1, source_target_pairs={{0,4},{1,5},{2,6},{3,7},{4,8},{5,9},{6,10},{7,11},{8,12},{9,13},{1... | collective-permute-start | bytes 1572872 | tf_op jit(solution)/shard_map/ppermute | solution.py:300
  36.6 16.3 %collective-permute-start.5 = (bf16[128,2048]{1,0:T(8,128)(2,1)S(1)}, bf16[128,2048]{1,0:T(8,128)(2,1)S(1)}, u32[]{:S(2)}, u32[]{:S(2)}) collective-permute-start(bf16[128,2048]{1,0:T(8,128)(2,1)S(1)} %all_gather.7.x0_ref), channel_id=1, source_target_pairs={{0,12},{1,13},{2,14},{3,15},{4,0},{5,1},{6,2},{7,3},{8,4},{9,5},{1... | collective-permute-start | bytes 1572872 | tf_op jit(solution)/shard_map/ppermute | solution.py:300
  44.3 24.0 %collective-permute-start.3 = (bf16[512,896]{1,0:T(8,128)(2,1)S(1)}, bf16[512,896]{1,0:T(8,128)(2,1)S(1)}, u32[]{:S(2)}, u32[]{:S(2)}) collective-permute-start(bf16[512,896]{1,0:T(8,128)(2,1)S(1)} %constant_dynamic-update-slice_fusion.near_ref), channel_id=1, source_target_pairs={{0,32},{32,64},{64,96},{96,128},{128,160},{160,192},{192,224},{224... | collective-permute-start | bytes 2752520 | tf_op jit(solution)/shard_map/ppermute | solution.py:294
  49.9 18.4 %collective-permute-start.7 = (bf16[512,896]{1,0:T(8,128)(2,1)S(1)}, bf16[512,896]{1,0:T(8,128)(2,1)S(1)}, u32[]{:S(2)}, u32[]{:S(2)}) collective-permute-start(bf16[512,896]{1,0:T(8,128)(2,1)S(1)} %constant_dynamic-update-slice_fusion.near_ref), channel_id=1, source_target_pairs={{0,16},{16,0},{32,48},{48,32},{64,80},{80,64},{96,112},{112,96},{1... | collective-permute-start | bytes 2752520 | tf_op jit(solution)/shard_map/ppermute | solution.py:297
  52.9 15.4 %collective-permute-start.6 = (bf16[128,2048]{1,0:T(8,128)(2,1)S(1)}, bf16[128,2048]{1,0:T(8,128)(2,1)S(1)}, u32[]{:S(2)}, u32[]{:S(2)}) collective-permute-start(bf16[128,2048]{1,0:T(8,128)(2,1)S(1)} %collective-permute-done.5.x3_ref), channel_id=1, source_target_pairs={{0,12},{1,13},{2,14},{3,15},{4,0},{5,1},{6,2},{7,3},{8,4},{9,5},{1... | collective-permute-start | bytes 1572872 | tf_op jit(solution)/shard_map/ppermute | solution.py:300
  56.3 17.8 %copy-start = (f32[4,256]{1,0:T(4,128)S(1)}, f32[4,256]{1,0:T(4,128)}, u32[]{:S(2)}) copy-start(f32[4,256]{1,0:T(4,128)} %tv_ref.1) | copy-start | bytes 12292
  56.3 17.8 %copy-start.1 = (s32[1,512]{1,0:T(1,128)S(1)}, s32[1,512]{1,0:T(1,128)}, u32[]{:S(2)}) copy-start(s32[1,512]{1,0:T(1,128)} %seg_ref.1) | copy-start | bytes 6148
  56.3 17.8 %copy-start.2 = (f32[4,128]{1,0:T(4,128)S(1)}, f32[4,128]{1,0:T(4,128)}, u32[]{:S(2)}) copy-start(f32[4,128]{1,0:T(4,128)} %tq_ref.1) | copy-start | bytes 6148
  56.3 17.8 %copy-start.3 = (f32[4,128]{1,0:T(4,128)S(1)}, f32[4,128]{1,0:T(4,128)}, u32[]{:S(2)}) copy-start(f32[4,128]{1,0:T(4,128)} %tk_ref.1) | copy-start | bytes 6148
  56.3 17.8 %copy-start.4 = (f32[2]{0:T(128)S(1)}, f32[2]{0:T(128)}, u32[]{:S(2)}) copy-start(f32[2]{0:T(128)} %rate_ref.1) | copy-start | bytes 28
  56.3 17.8 %copy-start.5 = (f32[2]{0:T(128)S(1)}, f32[2]{0:T(128)}, u32[]{:S(2)}) copy-start(f32[2]{0:T(128)} %bias_ref.1) | copy-start | bytes 28
  56.3 17.8 %copy-start.6 = (f32[128]{0:T(128)S(1)}, f32[128]{0:T(128)}, u32[]{:S(2)}) copy-start(f32[128]{0:T(128)} %param.28) | copy-start | bytes 1540
  56.4 10.7 %collective-permute-start.4 = (bf16[128,896]{1,0:T(8,128)(2,1)S(1)}, bf16[128,896]{1,0:T(8,128)(2,1)S(1)}, u32[]{:S(2)}, u32[]{:S(2)}) collective-permute-start(bf16[128,896]{1,0:T(8,128)(2,1)S(1)} %slice.4), channel_id=1, source_target_pairs={{0,64},{32,96},{64,128},{96,160},{128,192},{160,224},{192,256},{22... | collective-permute-start | bytes 688136 | tf_op jit(solution)/shard_map/ppermute | solution.py:294
  68.4 5.7 %collective-permute-start.8 = (bf16[512,896]{1,0:T(8,128)(2,1)S(1)}, bf16[512,896]{1,0:T(8,128)(2,1)S(1)}, u32[]{:S(2)}, u32[]{:S(2)}) collective-permute-start(bf16[512,896]{1,0:T(8,128)(2,1)S(1)} %collective-permute-done.3.far_ref), channel_id=1, source_target_pairs={{0,16},{16,0},{32,48},{48,32},{64,80},{80,64},{96,112},{112,96},{1... | collective-permute-start | bytes 2752520 | tf_op jit(solution)/shard_map/ppermute | solution.py:297
